TPU v7x, 128 devices: a whole 4x4x4 slice. The times are simulated.
128 devices in a mesh: dp: 32 (over z, x, core), mp: 4 (over y).
Axes of the slice: x: 4, y: 4, z: 4, core: 2. Of those that a mesh axis runs over, the one named last changes fastest.
Arguments:
- patch_rows: bfloat16 [32768, 1664], P(('dp', 'mp')), may hold values from -64 to 64
- packing: int32 [2, 32768], P(None, ('dp', 'mp')), may hold values from 0 to 255, as said below
- segment: int32 [32768], P('dp'), may hold values from 0 to 48, as said below
- coords: int32 [2, 32768], P(None, ('dp', 'mp')), may hold values from 0 to 15, as said below
- pos_rows: bfloat16 [16, 1664], replicated, may hold values from -3 to 3
- pos_cols: bfloat16 [16, 1664], replicated, may hold values from -3 to 3
- norm_gain: bfloat16 [1664], replicated, may hold values from 0.25 to 1.75
- w_qkv: bfloat16 [1664, 3, 1664], P(None, None, 'mp'), may hold values from -1.25 to 1.25
- w_out: bfloat16 [1664, 1664], P('mp'), may hold values from -0.4375 to 0.4375
- cotangent: bfloat16 [32768, 1664], P(('dp', 'mp')), may hold values from -6 to 6
Outputs:
- output: bfloat16 [32768, 1664], P(('dp', 'mp'))
- d_patches: bfloat16 [32768, 1664], P(('dp', 'mp'))
- grad_qkv: float32 [1664, 3, 1664], P(None, None, 'mp')
- grad_out: float32 [1664, 1664], P('mp')
Inputs may be any that keep to these rules, and one draw needn't show every extreme that they name: `packing`: each loader row goes to a device of the same mp index; every row of every device receives exactly one loader row. From one device to one device at most 16 rows go, and every device sends exactly 16 rows to one device. The counts from a device to the devices of its mp index form the same list on every device, in an order that differs from device to device. `segment`: within each packed sequence the image numbers start at 0 and rise by one from image to image; an image holds at most 256 patches, the first image of every sequence exactly that many, and every image but a sequence's last has at least 4 patch rows and columns. Some sequence holds as many images as fit. `coords`: patches of an image fill its grid row by row; the last image of a sequence may be cut short.
All inputs are finite; a program needn't handle non-finite values.
Results may differ from a plain program's by a relative error of at most 0.034.
Values may be sent and summed in bfloat16 or wider, within the bound.
A program may use at most 128 MiB of HBM per device.

v0:
```python
import jax
import jax.numpy as jnp
from jax import lax
from jax.sharding import PartitionSpec as P

HD = 104


def layer_norm(values):
    row_mean = jnp.mean(values, axis=-1, keepdims=True)
    centered = values - row_mean
    variance = jnp.mean(centered * centered, axis=-1, keepdims=True)
    inv_std = lax.rsqrt(variance + 1e-06)
    return (centered * inv_std, inv_std)


def local(
    patch_rows, packing, segment, coords, pos_rows, pos_cols, norm_gain, w_qkv, w_out, cotangent
):
    row_count = patch_rows.shape[0]
    model_width = patch_rows.shape[1]
    group_count = lax.axis_size("dp")
    lane_count = lax.axis_size("mp")
    capacity = 2 * row_count // group_count
    total_rows = row_count * lane_count * group_count
    coef = total_rows ** (-0.5)
    seq_rows = segment.shape[0]
    group_width = w_qkv.shape[2]
    local_heads = group_width // HD
    score_scale = HD ** (-0.5)
    dest_group = packing[0]
    dest_row = packing[1]
    onehot = (dest_group[:, None] == jnp.arange(group_count, dtype=jnp.int32)[None, :]).astype(
        jnp.int32
    )
    earlier = jnp.cumsum(onehot, axis=0) - onehot
    placed = dest_group * capacity + jnp.sum(earlier * onehot, axis=1)
    send_rows = (
        jnp.zeros((group_count * capacity, model_width), jnp.bfloat16).at[placed].set(patch_rows)
    )
    send_index = jnp.full((group_count * capacity,), row_count, jnp.int32).at[placed].set(dest_row)
    recv_rows, recv_index = (
        lax.all_to_all(send_rows, "dp", split_axis=0, concat_axis=0, tiled=True),
        lax.all_to_all(send_index, "dp", split_axis=0, concat_axis=0, tiled=True),
    )
    packed = (
        jnp.zeros((row_count, model_width), jnp.bfloat16).at[recv_index].set(recv_rows, mode="drop")
    )
    grid_size = pos_rows.shape[0]
    grid_range = jnp.arange(grid_size, dtype=jnp.int32)[None, :]
    row_hot = (coords[0][:, None] == grid_range).astype(jnp.bfloat16)
    col_hot = (coords[1][:, None] == grid_range).astype(jnp.bfloat16)
    stream = (
        packed.astype(jnp.float32)
        + jnp.dot(row_hot, pos_rows, preferred_element_type=jnp.float32)
        + jnp.dot(col_hot, pos_cols, preferred_element_type=jnp.float32)
    ).astype(jnp.bfloat16)
    stream_f = stream.astype(jnp.float32)
    unit, inv_std = layer_norm(stream_f)
    gain_f = norm_gain.astype(jnp.float32)
    normed = (unit * gain_f).astype(jnp.bfloat16)
    gathered = lax.all_gather(normed, "mp", axis=0, tiled=True)
    w_flat = w_qkv.reshape(model_width, 3 * group_width)
    qkv = jnp.dot(gathered, w_flat, preferred_element_type=jnp.float32).astype(jnp.bfloat16)
    query = qkv[:, :group_width].reshape(seq_rows, local_heads, HD)
    keys = qkv[:, group_width : 2 * group_width].reshape(seq_rows, local_heads, HD)
    values = qkv[:, 2 * group_width :].reshape(seq_rows, local_heads, HD)
    same_image = (segment[:, None] == segment[None, :])[None]
    scores = (
        jnp.einsum("qhd,khd->hqk", query, keys, preferred_element_type=jnp.float32) * score_scale
    )
    scores = jnp.where(same_image, scores, -1e30)
    row_max = jnp.max(scores, axis=-1, keepdims=True)
    expo = jnp.where(same_image, jnp.exp(scores - row_max), 0.0)
    prob = expo / jnp.sum(expo, axis=-1, keepdims=True)
    prob_b = prob.astype(jnp.bfloat16)
    attended = jnp.einsum(
        "hqk,khd->qhd", prob_b, values, preferred_element_type=jnp.float32
    ).astype(jnp.bfloat16)
    attended = attended.reshape(seq_rows, group_width)
    block_rows = attended
    attn_sum = lax.psum_scatter(
        jnp.dot(block_rows, w_out, preferred_element_type=jnp.float32).astype(jnp.bfloat16),
        "mp",
        scatter_dimension=0,
        tiled=True,
    ).astype(jnp.float32)
    output = (stream_f + attn_sum).astype(jnp.bfloat16)
    block_rows = lax.all_gather(cotangent, "mp", axis=0, tiled=True)
    out_acc = lax.dot_general(
        attended, block_rows, (((0,), (0,)), ((), ())), preferred_element_type=jnp.float32
    )
    d_rows = lax.dot_general(
        block_rows, w_out, (((1,), (1,)), ((), ())), preferred_element_type=jnp.float32
    )
    d_acc = d_rows
    d_acc, out_acc = (d_acc, out_acc)
    grad_out = out_acc * coef
    d_attended = d_acc.astype(jnp.bfloat16).reshape(seq_rows, local_heads, HD)
    att_heads = attended.reshape(seq_rows, local_heads, HD)
    delta = jnp.einsum("qhd,qhd->hq", d_attended, att_heads, preferred_element_type=jnp.float32)
    d_prob = jnp.einsum("qhd,khd->hqk", d_attended, values, preferred_element_type=jnp.float32)
    d_score = (prob * (d_prob - delta[:, :, None]) * score_scale).astype(jnp.bfloat16)
    d_query = jnp.einsum("hqk,khd->qhd", d_score, keys, preferred_element_type=jnp.float32).astype(
        jnp.bfloat16
    )
    d_key = jnp.einsum("hqk,qhd->khd", d_score, query, preferred_element_type=jnp.float32).astype(
        jnp.bfloat16
    )
    d_value = jnp.einsum(
        "hqk,qhd->khd", prob_b, d_attended, preferred_element_type=jnp.float32
    ).astype(jnp.bfloat16)
    d_qkv = jnp.concatenate(
        [
            d_query.reshape(seq_rows, group_width),
            d_key.reshape(seq_rows, group_width),
            d_value.reshape(seq_rows, group_width),
        ],
        axis=1,
    )
    grad_qkv = lax.dot_general(
        gathered, d_qkv, (((0,), (0,)), ((), ())), preferred_element_type=jnp.float32
    )
    grad_qkv = (grad_qkv * coef).reshape(model_width, 3, group_width)
    block_rows = d_qkv
    d_normed = lax.psum_scatter(
        lax.dot_general(
            block_rows, w_flat, (((1,), (1,)), ((), ())), preferred_element_type=jnp.float32
        ).astype(jnp.bfloat16),
        "mp",
        scatter_dimension=0,
        tiled=True,
    ).astype(jnp.float32)
    scaled = d_normed * gain_f
    d_stream = cotangent.astype(jnp.float32) + inv_std * (
        scaled
        - jnp.mean(scaled, axis=-1, keepdims=True)
        - unit * jnp.mean(scaled * unit, axis=-1, keepdims=True)
    )
    d_stream = d_stream.astype(jnp.bfloat16)
    valid_slot = (recv_index < row_count)[:, None]
    back_rows = jnp.where(
        valid_slot,
        jnp.take(d_stream, jnp.minimum(recv_index, row_count - 1), axis=0),
        jnp.zeros((), jnp.bfloat16),
    )
    returned = lax.all_to_all(back_rows, "dp", split_axis=0, concat_axis=0, tiled=True)
    d_patches = jnp.take(returned, placed, axis=0)
    grad_qkv, grad_out = (
        lax.psum(grad_qkv.astype(jnp.bfloat16), "dp").astype(jnp.float32),
        lax.psum(grad_out.astype(jnp.bfloat16), "dp").astype(jnp.float32),
    )
    return (output, d_patches, grad_qkv, grad_out)


def solution(mesh):
    placed = (
        P(("dp", "mp"), None),
        P(None, ("dp", "mp")),
        P("dp"),
        P(None, ("dp", "mp")),
        P(),
        P(),
        P(),
        P(None, None, "mp"),
        P("mp", None),
        P(("dp", "mp"), None),
    )
    return jax.shard_map(
        local,
        mesh=mesh,
        in_specs=placed,
        out_specs=(
            P(("dp", "mp"), None),
            P(("dp", "mp"), None),
            P(None, None, "mp"),
            P("mp", None),
        ),
        check_vma=False,
    )
```

profile of v0, /device:TPU:1, one launch (start us, length us, event | category | flops | bytes accessed | tf_op | source)
XLA Modules:
  0.0 395.8 jit_solution(7938538182130163143)
XLA Ops:
  12.4 9.4 %all-to-all-start = ((s32[32,16,1]{1,2,0:T(1,128)}), s32[32,16,1]{1,2,0:T(1,128)S(1)}, u32[]{:S(2)}, u32[]{:S(2)}) async-start(s32[32,16,1]{1,2,0:T(1,128)} %bitcast.9), calls=%async_computation | async-start | bytes 32768 | tf_op jit(solution)/shard_map/all_to_all | solution.py:44
  21.9 4.0 %scatter_custom_fusion.1 = bf16[512,1664]{1,0:T(8,128)(2,1)} fusion(s32[256]{0:T(256)S(1)} %bitcast.123, bf16[256,1664]{1,0:T(8,128)(2,1)} %param.10, bf16[]{:T(256)} %constant.20.clone.1), kind=kCustom, calls=%fused_computation.45 | custom fusion | bytes 1704448 | tf_op jit(solution)/shard_map/scatter | solution.py:39
  28.7 4.7 %all-to-all-start.1 = ((bf16[32,16,1664]{2,1,0:T(8,128)(2,1)}), bf16[32,16,1664]{2,1,0:T(8,128)(2,1)S(1)}, u32[]{:S(2)}, u32[]{:S(2)}) async-start(bf16[32,16,1664]{2,1,0:T(8,128)(2,1)} %bitcast.11), calls=%async_computation.1 | async-start | bytes 3407872 | tf_op jit(solution)/shard_map/all_to_all | solution.py:43
  34.8 22.1 %all-to-all-done.1 = bf16[32,16,1664]{2,1,0:T(8,128)(2,1)S(1)} async-done(((bf16[32,16,1664]{2,1,0:T(8,128)(2,1)}), bf16[32,16,1664]{2,1,0:T(8,128)(2,1)S(1)}, u32[]{:S(2)}, u32[]{:S(2)}) %all-to-all-start.1) | async-done | bytes 1703968 | tf_op jit(solution)/shard_map/all_to_all | solution.py:43
  58.0 4.2 %scatter_custom_fusion.2 = bf16[256,1664]{1,0:T(8,128)(2,1)S(1)} fusion(s32[512]{0:T(512)S(1)} %bitcast.125, bf16[512,1664]{1,0:T(8,128)(2,1)} %bitcast.105, bf16[]{:T(256)} %constant.20.clone.1), kind=kCustom, calls=%fused_computation.48 | custom fusion | bytes 852480 | tf_op jit(solution)/shard_map/scatter | solution.py:47
  67.1 4.6 %convolution_convert_fusion.6 = bf16[1024,416]{0,1:T(8,128)(2,1)} fusion(bf16[1024,1664]{1,0:T(8,128)(2,1)} %all-gather.5.cloned.1.call-done, bf16[416,1664]{1,0:T(8,128)(2,1)S(1)} %copy-done), kind=kOutput, calls=%fused_computation.43 | convolution fusion | flops 1418100736 | bytes 5644288 | tf_op jit(solution)/shard_map/dot_general | solution.py:93
  71.7 33.8 %all-gather.3.cloned.1.call-done = bf16[1024,1664]{1,0:T(8,128)(2,1)} async-done(((bf16[256,1664]{1,0:T(8,128)(2,1)}), bf16[1024,1664]{1,0:T(8,128)(2,1)}) %all-gather.3.cloned.1.call-update) | async-done | bytes 3407888 | tf_op jit(solution)/shard_map/all_gather | solution.py:62
  105.4 8.0 %convolution_convert_fusion.1 = bf16[1024,1248]{0,1:T(8,128)(2,1)S(1)} fusion(bf16[1024,1664]{1,0:T(8,128)(2,1)} %all-gather.3.cloned.1.call-done, bf16[1664,1248]{0,1:T(8,128)(2,1)} %bitcast.127), kind=kOutput, calls=%fused_computation.18 | convolution fusion | flops 4254302208 | bytes 10117120 | tf_op jit(solution)/shard_map/dot_general | solution.py:64
  115.0 13.6 %fusion.34 = (f32[4,1024]{1,0:T(4,128)S(1)}, f32[4,1024,1024]{1,2,0:T(8,128)}) fusion(pred[1024,1024]{0,1:T(8,128)(4,1)} %broadcast_compare_fusion, bf16[1024,4,104]{0,2,1:T(8,128)(2,1)} %bitcast.98, bf16[1024,4,104]{0,2,1:T(8,128)(2,1)} %bitcast.96), kind=kOutput, calls=%fused_computation.89 | convolution fusion | flops 893387776 | bytes 19546112 | tf_op jit(solution)/shard_map/sub | solution.py:74
  128.6 7.0 %fusion.6 = bf16[4,1024,1024]{1,2,0:T(8,128)(2,1)S(1)} fusion(f32[4,1024,1024]{1,2,0:T(8,128)} %get-tuple-element.24, f32[4,1024]{1,0:T(4,128)S(1)} %get-tuple-element.23), kind=kLoop, calls=%fused_computation.16 | loop fusion | flops 8388608 | bytes 25182208 | tf_op jit(solution)/shard_map/convert_element_type | solution.py:76
  140.9 7.6 %multiply_convert_fusion = bf16[4,1024,1024]{1,2,0:T(8,128)(2,1)S(1)} fusion(bf16[1024,4,104]{0,2,1:T(8,128)(2,1)S(1)} %bitcast.102, bf16[1024,4,104]{0,2,1:T(8,128)(2,1)S(1)} %bitcast.104, f32[4,1024]{1,0:T(4,128)S(1)} %get-tuple-element.25, f32[4,1024,1024]{1,2,0:T(8,128)} %get-tuple-element.24, f32[4,1024]{1,0:T(4,128)S(1)} %get-tuple-element.23), kind=kOutput, calls=%fused_computation.6 | convolution fusion | flops 893386752 | bytes 26902528 | tf_op jit(solution)/shard_map/qhd,khd->hqk/dot_general | solution.py:102
  154.0 6.4 %convolution_convert_fusion = bf16[1024,1664]{1,0:T(8,128)(2,1)} fusion(bf16[1664,1248]{0,1:T(8,128)(2,1)S(1)} %bitcast.128, bf16[1024,416]{0,1:T(8,128)(2,1)S(1)} %bitcast.106, bf16[1024,416]{0,1:T(8,128)(2,1)S(1)} %bitcast.108, bf16[1024,416]{0,1:T(8,128)(2,1)S(1)} %bitcast.110), kind=kOutput, calls=%fused_computation.17 | convolution fusion | flops 4262395904 | bytes 10117120 | tf_op jit(solution)/shard_map/dot_general | solution.py:127
  160.5 5.1 %convolution_convert_fusion.2 = bf16[1024,1664]{1,0:T(8,128)(2,1)} fusion(bf16[1024,416]{0,1:T(8,128)(2,1)} %bitcast.112, bf16[416,1664]{1,0:T(8,128)(2,1)S(1)} %copy-done), kind=kOutput, calls=%fused_computation.19 | convolution fusion | flops 1419378688 | bytes 5644288 | tf_op jit(solution)/shard_map/dot_general | solution.py:83
  165.9 5.2 %fusion.7 = bf16[416,1664]{1,0:T(8,128)(2,1)} fusion(bf16[1024,416]{0,1:T(8,128)(2,1)} %bitcast.113, bf16[1024,1664]{1,0:T(8,128)(2,1)} %all-gather.5.cloned.1.call-done), kind=kOutput, calls=%fused_computation.21 | convolution fusion | flops 1419059200 | bytes 5644288 | tf_op jit(solution)/shard_map/dot_general | solution.py:90
  171.1 8.3 %fusion.5 = bf16[1664,1248]{0,1:T(8,128)(2,1)} fusion(bf16[1024,1664]{1,0:T(8,128)(2,1)S(1)} %copy-done.20, bf16[1024,416]{0,1:T(8,128)(2,1)S(1)} %bitcast.107, bf16[1024,416]{0,1:T(8,128)(2,1)S(1)} %bitcast.109, bf16[1024,416]{0,1:T(8,128)(2,1)S(1)} %bitcast.111), kind=kOutput, calls=%fused_computation.15 | convolution fusion | flops 4264845312 | bytes 10117120 | tf_op jit(solution)/shard_map/dot_general | solution.py:121
  179.4 21.9 %reduce-scatter.5.cloned.1.call-done = bf16[256,1664]{1,0:T(8,128)(2,1)} async-done(((bf16[1024,1664]{1,0:T(8,128)(2,1)}), bf16[256,1664]{1,0:T(8,128)(2,1)}) %reduce-scatter.5.cloned.1.call-update) | async-done | bytes 851984 | tf_op jit(solution)/shard_map/reduce_scatter | solution.py:126
  203.0 40.7 %reduce-scatter.3.cloned.1.call-done = bf16[256,1664]{1,0:T(8,128)(2,1)} async-done(((bf16[1024,1664]{1,0:T(8,128)(2,1)}), bf16[256,1664]{1,0:T(8,128)(2,1)}) %reduce-scatter.3.cloned.1.call-update) | async-done | bytes 851984 | tf_op jit(solution)/shard_map/reduce_scatter | solution.py:82
  243.7 3.9 add_convert_fusion
  247.6 3.1 gather_fusion
  250.7 3.0 select_select_fusion
  253.7 7.6 %all-to-all-start.2 = ((bf16[32,16,1664]{2,1,0:T(8,128)(2,1)}), bf16[32,16,1664]{2,1,0:T(8,128)(2,1)S(1)}, u32[]{:S(2)}, u32[]{:S(2)}) async-start(bf16[32,16,1664]{2,1,0:T(8,128)(2,1)} %select_select_fusion), calls=%async_computation.4 | async-start | bytes 3407872 | tf_op jit(solution)/shard_map/all_to_all | solution.py:147
  261.4 116.0 %all-reduce.3.cloned.1.call-done = (bf16[1664,3,416]{0,2,1:T(8,128)(2,1)}, bf16[416,1664]{1,0:T(8,128)(2,1)}) async-done(((bf16[1664,3,416]{0,2,1:T(8,128)(2,1)}, bf16[416,1664]{1,0:T(8,128)(2,1)}), (bf16[1664,3,416]{0,2,1:T(8,128)(2,1)}, bf16[416,1664]{1,0:T(8,128)(2,1)})) %all-reduce.3.cloned.1.call-update) | async-done | bytes 5537808 | tf_op jit(solution)/shard_map/psum | solution.py:150
  377.4 3.2 convert_element_type.126
  380.6 3.9 convert_element_type.124
  (94 shorter events, 34.0 us)
Async XLA Ops:
  7.2 59.9 %copy-start = (bf16[416,1664]{1,0:T(8,128)(2,1)S(1)}, bf16[416,1664]{1,0:T(8,128)(2,1)}, u32[]{:S(2)}) copy-start(bf16[416,1664]{1,0:T(8,128)(2,1)} %param.18) | copy-start | bytes 4153348
  7.2 59.9 %all-gather.5.cloned.1.call-start = ((), (), s32[]{:S(2)}) async-start(), calls=%async_computation.7 | async-start | bytes 4259840 | tf_op jit(solution)/shard_map/all_gather | solution.py:89
  12.4 16.3 %all-to-all-start = ((s32[32,16,1]{1,2,0:T(1,128)}), s32[32,16,1]{1,2,0:T(1,128)S(1)}, u32[]{:S(2)}, u32[]{:S(2)}) async-start(s32[32,16,1]{1,2,0:T(1,128)} %bitcast.9), calls=%async_computation | async-start | bytes 32768 | tf_op jit(solution)/shard_map/all_to_all | solution.py:44
  21.8 11.6 %copy-start.17 = (bf16[1664]{0:T(1024)(128)(2,1)S(1)}, bf16[1664]{0:T(1024)(128)(2,1)}, u32[]{:S(2)}) copy-start(bf16[1664]{0:T(1024)(128)(2,1)} %param.16) | copy-start | bytes 9988
  21.8 11.6 %copy-start.18 = (s32[2,256]{1,0:T(2,128)S(1)}, s32[2,256]{1,0:T(2,128)}, u32[]{:S(2)}) copy-start(s32[2,256]{1,0:T(2,128)} %param.13) | copy-start | bytes 6148
  25.8 36.4 %copy-start.14 = (bf16[16,1664]{1,0:T(8,128)(2,1)S(1)}, bf16[16,1664]{1,0:T(8,128)(2,1)}, u32[]{:S(2)}) copy-start(bf16[16,1664]{1,0:T(8,128)(2,1)} %param.14) | copy-start | bytes 159748
  28.7 28.2 %all-to-all-start.1 = ((bf16[32,16,1664]{2,1,0:T(8,128)(2,1)}), bf16[32,16,1664]{2,1,0:T(8,128)(2,1)S(1)}, u32[]{:S(2)}, u32[]{:S(2)}) async-start(bf16[32,16,1664]{2,1,0:T(8,128)(2,1)} %bitcast.11), calls=%async_computation.1 | async-start | bytes 3407872 | tf_op jit(solution)/shard_map/all_to_all | solution.py:43
  33.4 29.3 %copy-start.15 = (bf16[16,1664]{1,0:T(8,128)(2,1)S(1)}, bf16[16,1664]{1,0:T(8,128)(2,1)}, u32[]{:S(2)}) copy-start(bf16[16,1664]{1,0:T(8,128)(2,1)} %param.15) | copy-start | bytes 159748
  33.4 72.0 %all-gather.3.cloned.1.call-start = ((), (), s32[]{:S(2)}) async-start(), calls=%async_computation.5 | async-start | bytes 4259840 | tf_op jit(solution)/shard_map/all_gather | solution.py:62
  63.2 138.0 %copy-start.1 = (f32[256,1664]{1,0:T(8,128)}, f32[256,1664]{1,0:T(8,128)S(1)}, u32[]{:S(2)}) copy-start(f32[256,1664]{1,0:T(8,128)S(1)} %get-tuple-element.22) | copy-start | bytes 5111812
  64.8 136.4 %reduce-scatter.5.cloned.1.call-start = ((), (), s32[]{:S(2)}) async-start(), calls=%async_computation.8 | async-start | bytes 4259840 | tf_op jit(solution)/shard_map/reduce_scatter | solution.py:126
  128.6 7.0 %copy-start.5 = (bf16[1024,416]{0,1:T(8,128)(2,1)S(1)}, bf16[1024,416]{0,1:T(8,128)(2,1)}, u32[]{:S(2)}) copy-start(bf16[1024,416]{0,1:T(8,128)(2,1)} %convolution_convert_fusion.6) | copy-start | bytes 2555908
  135.7 2.7 copy-start.6
  138.4 14.2 %copy-start.8 = (bf16[4,104,1024]{2,1,0:T(8,128)(2,1)}, bf16[4,104,1024]{2,1,0:T(8,128)(2,1)S(1)}, u32[]{:S(2)}) copy-start(bf16[4,104,1024]{2,1,0:T(8,128)(2,1)S(1)} %convolution_convert_fusion.3) | copy-start | bytes 2555908
  140.9 7.6 %copy-start.4 = (bf16[1024,416]{0,1:T(8,128)(2,1)S(1)}, bf16[1024,416]{0,1:T(8,128)(2,1)}, u32[]{:S(2)}) copy-start(bf16[1024,416]{0,1:T(8,128)(2,1)} %get-tuple-element.9) | copy-start | bytes 2555908
  151.2 2.8 copy-start.19
  160.4 83.2 %reduce-scatter.3.cloned.1.call-start = ((), (), s32[]{:S(2)}) async-start(), calls=%async_computation.6 | async-start | bytes 4259840 | tf_op jit(solution)/shard_map/reduce_scatter | solution.py:82
  165.6 211.8 %all-reduce.3.cloned.1.call-start = ((), (), s32[]{:S(2)}) async-start(), calls=%async_computation.9 | async-start | bytes 11075584 | tf_op jit(solution)/shard_map/psum | solution.py:150
  165.9 5.2 %copy-start.9 = (bf16[4,104,1024]{2,1,0:T(8,128)(2,1)S(1)}, bf16[4,104,1024]{2,1,0:T(8,128)(2,1)}, u32[]{:S(2)}) copy-start(bf16[4,104,1024]{2,1,0:T(8,128)(2,1)} %copy-done.8) | copy-start | bytes 2555908
  165.9 5.2 %copy-start.11 = (bf16[4,104,1024]{2,1,0:T(8,128)(2,1)S(1)}, bf16[4,104,1024]{2,1,0:T(8,128)(2,1)}, u32[]{:S(2)}) copy-start(bf16[4,104,1024]{2,1,0:T(8,128)(2,1)} %copy-done.10) | copy-start | bytes 2555908
  165.9 5.2 %copy-start.13 = (bf16[4,104,1024]{2,1,0:T(8,128)(2,1)S(1)}, bf16[4,104,1024]{2,1,0:T(8,128)(2,1)}, u32[]{:S(2)}) copy-start(bf16[4,104,1024]{2,1,0:T(8,128)(2,1)} %copy-done.12) | copy-start | bytes 2555908
  165.9 5.2 %copy-start.20 = (bf16[1024,1664]{1,0:T(8,128)(2,1)S(1)}, bf16[1024,1664]{1,0:T(8,128)(2,1)}, u32[]{:S(2)}) copy-start(bf16[1024,1664]{1,0:T(8,128)(2,1)} %all-gather.3.cloned.1.call-done) | copy-start | bytes 10223620
  253.7 130.8 %all-to-all-start.2 = ((bf16[32,16,1664]{2,1,0:T(8,128)(2,1)}), bf16[32,16,1664]{2,1,0:T(8,128)(2,1)S(1)}, u32[]{:S(2)}, u32[]{:S(2)}) async-start(bf16[32,16,1664]{2,1,0:T(8,128)(2,1)} %select_select_fusion), calls=%async_computation.4 | async-start | bytes 3407872 | tf_op jit(solution)/shard_map/all_to_all | solution.py:147
  377.4 3.2 copy-start.2
  (5 other events, 8.4 us)
Sparse Core Ops, SparseCore 0:
  9.7 44.9 all-gather.4
  65.0 40.4 all-gather.2
  160.6 40.6 reduce-scatter.4
  203.5 40.0 reduce-scatter.2
  247.7 129.6 all-reduce.2
where the time goes:
time: 403 us; the launch traced here: 396 us
  waiting for transfers between devices  238 us (59%)
  matrix products  68.9 us (17%)
  other arithmetic  30.3 us (8%)
  starting transfers between devices  22.4 us (6%)
  local copies, waits for them, and re-layouts  21.5 us (5%)
  between operations  14.5 us (4%)
    psum x1, waiting for transfers between devices, local(): lax.psum(grad_qkv.astype(jnp.bfloat16), 'dp').astype(jnp.float32)  116 us
    reduce_scatter x1, waiting for transfers between devices, local(): lax.psum_scatter(jnp.dot(block_rows, w_out, preferred_element_type=jnp.fl...  40.7 us
    all_gather x1, waiting for transfers between devices, local(): gathered = lax.all_gather(normed, 'mp', axis=0, tiled=True)  33.8 us
    all_to_all x1, waiting for transfers between devices, local(): lax.all_to_all(send_rows, 'dp', split_axis=0, concat_axis=0, tiled=True)  22.1 us
    reduce_scatter x1, waiting for transfers between devices, local(): lax.psum_scatter(lax.dot_general(block_rows, w_flat, (((1,), (1,)), ((),...  21.9 us
    sub x1, matrix products, local(): expo = jnp.where(same_image, jnp.exp(scores - row_max), 0.0)  13.6 us
    all_to_all x1, starting transfers between devices, local(): lax.all_to_all(send_index, 'dp', split_axis=0, concat_axis=0, tiled=True)  9.43 us
    dot_general x1, matrix products, local(): lax.dot_general(gathered, d_qkv, (((0,), (0,)), ((), ())), preferred_elem...  8.27 us
  transfers between devices with their start and end apart: 8, of which 6 were waited for; matrix products, arithmetic and copies ran while one was open for 15% of the time, Pallas kernels for 0%

commit v1 on v0

v1 whole, which is shorter than its diff:
```python
import jax
import jax.numpy as jnp
from jax import lax
from jax.experimental import pallas as pl
from jax.experimental.pallas import tpu as pltpu
from jax.sharding import PartitionSpec as P

HD = 104
HP = 128
NH = 4
D = 1664
RD = 256
SEQ = 1024
CAP = 16
NDP = 32
SLOTS = NDP * CAP
CA = 896
MESH = pl.DeviceIdType.MESH
F32 = jnp.float32
BF = jnp.bfloat16
VM = pl.BlockSpec(memory_space=pltpu.VMEM)
BLOCKS = ((0, 0, 256, 0), (256, 256, 768, 256), (512, 256, 1024, 768), (768, 512, 1024, 1536))


def mm(a, b, ca=1, cb=0):
    return lax.dot_general(a, b, (((ca,), (cb,)), ((), ())), preferred_element_type=F32)


def rows(start, size):
    return pl.ds(pl.multiple_of(start, 16), size)


def place():
    dp, mp = lax.axis_index("dp"), lax.axis_index("mp")
    return dp, mp, lax.rem(mp + 1, 4), lax.rem(mp + 3, 4), lax.rem(mp + 2, 4)


def copier(ssem, rsem):
    def make(src, dst, n, dev):
        return pltpu.make_async_remote_copy(
            src, dst, ssem.at[n], rsem.at[n], device_id=dev, device_id_type=MESH
        )

    return make


def greet(devs):
    bar = pltpu.get_barrier_semaphore()
    for dev in devs:
        pl.semaphore_signal(bar, inc=1, device_id=dev, device_id_type=MESH)
    return bar


def greet_dp(dp, mp, right, left):
    bar = greet(((dp, right), (dp, left)))

    def one(i, carry):
        pl.semaphore_signal(
            bar, inc=1, device_id=(lax.rem(dp + i, NDP), mp), device_id_type=MESH
        )
        return carry

    lax.fori_loop(1, NDP, one, 0)
    return bar


def a2a_copies(src, dst, ssem, rsem, dp, mp):
    def make(i):
        d = lax.rem(dp + i, NDP)
        return pltpu.make_async_remote_copy(
            src.at[rows(d * CAP, CAP)],
            dst.at[rows(dp * CAP, CAP)],
            ssem.at[i],
            rsem.at[i],
            device_id=(d, mp),
            device_id_type=MESH,
        )

    def start():
        def one(i, carry):
            make(i).start()
            return carry

        lax.fori_loop(1, NDP, one, 0)
        dst[rows(dp * CAP, CAP)] = src[rows(dp * CAP, CAP)]

    def wait():
        def one(i, carry):
            make(i).wait()
            return carry

        lax.fori_loop(1, NDP, one, 0)

    return start, wait


def ring_gather(src, dst, ssem, rsem, dp, mp, right, left):
    make = copier(ssem, rsem)
    h = RD // 2

    def at(dev, half):
        return dst.at[rows(dev * RD + half * h, h)]

    a0 = make(src.at[0:h], at(mp, 0), 0, (dp, right))
    b1 = make(src.at[h:RD], at(mp, 1), 1, (dp, left))
    a1 = make(src.at[h:RD], at(mp, 1), 2, (dp, right))
    b0 = make(src.at[0:h], at(mp, 0), 3, (dp, left))
    f0 = make(at(left, 0), at(left, 0), 4, (dp, right))
    f1 = make(at(right, 1), at(right, 1), 5, (dp, left))

    def start():
        for c in (a0, b1, a1, b0):
            c.start()

    def onward():
        a0.wait_recv()
        f0.start()
        b1.wait_recv()
        f1.start()

    def near():
        a1.wait_recv()
        b0.wait_recv()

    def far():
        f0.wait_recv()
        f1.wait_recv()

    def drain():
        for c in (a0, b1, a1, b0, f0, f1):
            c.wait_send()

    return start, onward, near, far, drain


def dispatch_kernel(
    patch, pack_col, pack_row, coords, pos, gain, wq, wo, cot,
    stream, ng, cotg, qkv, datt, idx, sel,
    send, recv, as_, ar, cs, cr, ns, nr,
):
    dp, mp, right, left, opp = place()
    bar = greet_dp(dp, mp, right, left)
    g_col, g_row = pack_col[:, 0:1], pack_row[0:1, :]
    src_i = lax.broadcasted_iota(jnp.int32, (RD, RD), 0)
    dst_i = lax.broadcasted_iota(jnp.int32, (RD, RD), 1)
    before = jnp.where((g_col == g_row) & (src_i < dst_i), 1.0, 0.0)
    rank = jnp.sum(before, axis=0, keepdims=True).astype(jnp.int32)
    placed = g_row * CAP + rank
    ext = jnp.broadcast_to((pack_col[:, 1:2] + 1).astype(F32), (RD, 128)).astype(BF)

    def fill(i, carry):
        at = rows(i * 128, 128)
        slot = lax.broadcasted_iota(jnp.int32, (128, RD), 0) + i * 128
        pick = jnp.where(slot == placed, 1.0, 0.0).astype(BF)
        sel[at, :] = pick
        send[at, 0:D] = mm(pick, patch[...]).astype(BF)
        send[at, D:] = mm(pick, ext).astype(BF)
        return carry

    lax.fori_loop(0, SLOTS // 128, fill, 0)
    pl.semaphore_wait(bar, NDP + 1)
    go, done = a2a_copies(send, recv, as_, ar, dp, mp)
    c_start, c_onward, c_near, c_far, c_drain = ring_gather(
        cot, cotg, cs, cr, dp, mp, right, left
    )
    go()
    c_start()
    cotg[rows(mp * RD, RD)] = cot[...]
    c_onward()
    done()
    code = recv[:, D:].astype(F32)
    idx[...] = recv[:, D:]

    def unpack(i, carry):
        at = rows(i * 64, 64)
        want = (lax.broadcasted_iota(jnp.int32, (SLOTS, 128), 1) + 1).astype(F32)
        pick = jnp.where(code == want + (i * 128).astype(F32), 1.0, 0.0).astype(BF)
        at = rows(i * 128, 128)
        packed = mm(pick, recv[:, 0:D], 0, 0)
        gi = lax.broadcasted_iota(jnp.int32, (128, 32), 1)
        cr_ = coords[at, 0:1]
        cc_ = coords[at, 1:2] + 16
        hot = jnp.where((gi == cr_) | (gi == cc_), 1.0, 0.0).astype(BF)
        s = (packed.astype(BF).astype(F32) + mm(hot, pos[...])).astype(BF)
        stream[at, :] = s
        sf = s.astype(F32)
        cen = sf - jnp.mean(sf, axis=-1, keepdims=True)
        inv = lax.rsqrt(jnp.mean(cen * cen, axis=-1, keepdims=True) + 1e-06)
        ng[rows(mp * RD + i * 128, 128), :] = (cen * inv * gain[...].astype(F32)).astype(BF)
        return carry

    lax.fori_loop(0, RD // 128, unpack, 0)
    n_start, n_onward, n_near, n_far, n_drain = ring_gather(
        ng.at[rows(mp * RD, RD)], ng, ns, nr, dp, mp, right, left
    )
    n_start()

    def project(s):
        def one(n, carry):
            col = pl.ds(pl.multiple_of(n * 512, 128), 512)
            qkv[rows(s * RD, RD), col] = mm(ng[rows(s * RD, RD)], wq[:, col]).astype(BF)
            return carry

        lax.fori_loop(0, 3, one, 0)

    def back(s):
        datt[rows(s * RD, RD), :] = mm(cotg[rows(s * RD, RD)], wo[...], 1, 1).astype(BF)

    project(mp)
    back(mp)
    c_near()
    c_far()
    n_onward()
    back(right)
    back(left)
    back(opp)
    n_near()
    project(right)
    project(left)
    n_far()
    project(opp)
    c_drain()
    n_drain()


def ring_reduce(part, ha, hb, fl, fr, ssem, rsem, dp, mp, right, left, opp):
    make = copier(ssem, rsem)
    h = RD // 2

    def at(dev, half):
        return part.at[rows(dev * RD + half * h, h)]

    s0 = make(at(opp, 0), ha, 0, (dp, right))
    s1 = make(at(opp, 1), hb, 1, (dp, left))
    s2 = make(at(right, 1), fl.at[h:RD], 2, (dp, right))
    s3 = make(at(left, 0), fr.at[0:h], 3, (dp, left))
    s4 = make(at(right, 0), fl.at[0:h], 4, (dp, right))
    s5 = make(at(left, 1), fr.at[h:RD], 5, (dp, left))

    def first():
        s0.start()
        s1.start()

    def second():
        s2.start()
        s3.start()

    def onward():
        s0.wait_recv()
        r0 = rows(right * RD, h)
        part[r0] = (part[r0].astype(F32) + ha[...].astype(F32)).astype(BF)
        s4.start()
        s1.wait_recv()
        r1 = rows(left * RD + h, h)
        part[r1] = (part[r1].astype(F32) + hb[...].astype(F32)).astype(BF)
        s5.start()

    def finish():
        for c in (s2, s3, s4, s5):
            c.wait_recv()

    def drain():
        for c in (s0, s1, s2, s3, s4, s5):
            c.wait_send()

    return first, second, onward, finish, drain


def attention_kernel(
    scal, qkv, datt, ng, cotg, seg_col, seg_row, wq, wo, stream,
    grad, dnp, out,
    prob, att, dqkv, dk, dv, part, ha, hb, fl, fr, ss, sr,
):
    dp, mp, right, left, opp = place()
    bar = greet(((dp, right), (dp, left)))
    scale = HD ** (-0.5)
    coef = scal[0]

    def fwd(h, carry):
        base = h * 3 * HP
        qc = pl.ds(pl.multiple_of(base, 128), HP)
        kc = pl.ds(pl.multiple_of(base + HP, 128), HP)
        vc = pl.ds(pl.multiple_of(base + 2 * HP, 128), HP)
        for r0, k0, k1, p0 in BLOCKS:
            s = mm(qkv[r0 : r0 + 256, qc], qkv[k0:k1, kc], 1, 1) * scale
            same = seg_col[r0 : r0 + 256, :] == seg_row[:, k0:k1]
            s = jnp.where(same, s, -1e30)
            e = jnp.where(same, jnp.exp(s - jnp.max(s, axis=-1, keepdims=True)), 0.0)
            p = (e / jnp.sum(e, axis=-1, keepdims=True)).astype(BF)
            prob[h, :, p0 : p0 + k1 - k0] = p
            hc = pl.ds(pl.multiple_of(h * HP, 128), HP)
            att[r0 : r0 + 256, hc] = mm(p, qkv[k0:k1, vc]).astype(BF)
        return carry

    lax.fori_loop(0, NH, fwd, 0)
    first, second, onward, finish, drain = ring_reduce(
        part, ha, hb, fl, fr, ss, sr, dp, mp, right, left, opp
    )

    def project(s):
        part[rows(s * RD, RD), :] = mm(att[rows(s * RD, RD), :], wo[...]).astype(BF)

    project(opp)
    pl.semaphore_wait(bar, 2)
    first()
    project(right)
    project(left)
    second()
    project(mp)

    def bwd(h, carry):
        base = h * 3 * HP
        qc = pl.ds(pl.multiple_of(base, 128), HP)
        kc = pl.ds(pl.multiple_of(base + HP, 128), HP)
        vc = pl.ds(pl.multiple_of(base + 2 * HP, 128), HP)
        hc = pl.ds(pl.multiple_of(h * HP, 128), HP)
        dk[...] = jnp.zeros_like(dk)
        dv[...] = jnp.zeros_like(dv)
        for r0, k0, k1, p0 in BLOCKS:
            p = prob[h, :, p0 : p0 + k1 - k0]
            da = datt[r0 : r0 + 256, hc]
            delta = jnp.sum(
                da.astype(F32) * att[r0 : r0 + 256, hc].astype(F32), axis=-1, keepdims=True
            )
            dprob = mm(da, qkv[k0:k1, vc], 1, 1)
            ds = (p.astype(F32) * (dprob - delta) * scale).astype(BF)
            dqkv[r0 : r0 + 256, qc] = mm(ds, qkv[k0:k1, kc]).astype(BF)
            dk[k0:k1, :] += mm(ds, qkv[r0 : r0 + 256, qc], 0, 0)
            dv[k0:k1, :] += mm(p, da, 0, 0)
        dqkv[:, kc] = dk[...].astype(BF)
        dqkv[:, vc] = dv[...].astype(BF)
        all3 = pl.ds(pl.multiple_of(base, 128), 3 * HP)
        grad[rows(h * 512, 384), :] = (mm(dqkv[:, all3], ng[...], 0, 0) * coef).astype(BF)
        grad[rows(h * 512 + 384, 128), :] = (mm(att[:, hc], cotg[...], 0, 0) * coef).astype(BF)

        @pl.when(h == 1)
        def _():
            onward()

        return carry

    lax.fori_loop(0, NH, bwd, 0)

    def d_rows(s, carry):
        dnp[rows(s * RD, RD), :] = mm(dqkv[rows(s * RD, RD), :], wq[...], 1, 1).astype(BF)
        return carry

    lax.fori_loop(0, 4, d_rows, 0)
    finish()
    total = part[rows(mp * RD, RD)].astype(F32) + fl[...].astype(F32) + fr[...].astype(F32)
    out[...] = (stream[...].astype(F32) + total).astype(BF)
    drain()


def reduce_kernel(
    grad, dnp_in, stream, cot, idx, sel, gain,
    total, dpatch,
    dnp, ha, hb, fl, fr, core_in, mine, ax, az, bx, bz, asum, bsum, back, ret, dstream,
    ys, yr, gs, gr, as_, ar,
):
    dp, mp, right, left, opp = place()
    bar = greet_dp(dp, mp, right, left)
    c = lax.rem(dp, 2)
    x = lax.rem(dp // 2, 4)
    z = dp // 8
    make = copier(gs, gr)
    other = 1 - c

    def dev(zz, xx, cc):
        return ((zz * 4 + xx) * 2 + cc, mp)

    def shift(v, s):
        return lax.rem(v + s, 4)

    dnp[...] = dnp_in[...]
    pl.semaphore_wait(bar, NDP + 1)
    first, second, onward, finish, drain = ring_reduce(
        dnp, ha, hb, fl, fr, ys, yr, dp, mp, right, left, opp
    )
    first()
    second()
    swap = make(grad.at[rows(other * 1024, 1024)], core_in, 0, dev(z, x, other))
    swap.start()
    swap.wait_recv()

    def add_core(i, carry):
        r = rows(i * 128, 128)
        g = grad[rows(c * 1024 + i * 128, 128)].astype(F32)
        mine[r, :] = (g + core_in[r, :].astype(F32)).astype(BF)
        return carry

    lax.fori_loop(0, 8, add_core, 0)
    a_cols, b_cols = pl.ds(0, CA), pl.ds(CA, D - CA)
    a1 = [make(mine.at[rows(shift(x, s) * 256, 256), a_cols], ax.at[s - 1], s, dev(z, shift(x, s), c)) for s in (1, 2, 3)]
    b1 = [make(mine.at[rows(shift(z, s) * 256, 256), b_cols], bx.at[s - 1], 3 + s, dev(shift(z, s), x, c)) for s in (1, 2, 3)]
    for s in (1, 0, 2):
        a1[s].start()
        b1[s].start()
    onward()
    for q in a1:
        q.wait_recv()
    asum[...] = (
        mine[rows(x * 256, 256), a_cols].astype(F32)
        + ax[0].astype(F32)
        + ax[1].astype(F32)
        + ax[2].astype(F32)
    ).astype(BF)
    a2 = [make(asum.at[rows(shift(z, s) * 64, 64)], az.at[s - 1], 6 + s, dev(shift(z, s), x, c)) for s in (1, 2, 3)]
    for q in a2:
        q.start()
    for q in b1:
        q.wait_recv()
    bsum[...] = (
        mine[rows(z * 256, 256), b_cols].astype(F32)
        + bx[0].astype(F32)
        + bx[1].astype(F32)
        + bx[2].astype(F32)
    ).astype(BF)
    b2 = [make(bsum.at[rows(shift(x, s) * 64, 64)], bz.at[s - 1], 9 + s, dev(z, shift(x, s), c)) for s in (1, 2, 3)]
    for q in b2:
        q.start()
    for q in a2:
        q.wait_recv()
    ra = rows(c * 1024 + x * 256 + z * 64, 64)
    total[ra, a_cols] = (
        asum[rows(z * 64, 64), :].astype(F32)
        + az[0].astype(F32)
        + az[1].astype(F32)
        + az[2].astype(F32)
    ).astype(BF)
    pa = total.at[ra, a_cols]
    a3 = [make(pa, pa, 12 + s, dev(shift(z, s), x, c)) for s in (1, 2, 3)]
    for q in a3:
        q.start()
    for q in b2:
        q.wait_recv()
    rb = rows(c * 1024 + z * 256 + x * 64, 64)
    total[rb, b_cols] = (
        bsum[rows(x * 64, 64), :].astype(F32)
        + bz[0].astype(F32)
        + bz[1].astype(F32)
        + bz[2].astype(F32)
    ).astype(BF)
    pb = total.at[rb, b_cols]
    b3 = [make(pb, pb, 15 + s, dev(z, shift(x, s), c)) for s in (1, 2, 3)]
    for q in b3:
        q.start()

    finish()
    go, done = a2a_copies(back, ret, as_, ar, dp, mp)

    def ln_back(i, carry):
        r = rows(i * 64, 64)
        sf = stream[r, :].astype(F32)
        cen = sf - jnp.mean(sf, axis=-1, keepdims=True)
        inv = lax.rsqrt(jnp.mean(cen * cen, axis=-1, keepdims=True) + 1e-06)
        unit = cen * inv
        dn = dnp[rows(mp * RD + i * 64, 64), :].astype(F32)
        e = (dn + fl[r, :].astype(F32) + fr[r, :].astype(F32)) * gain[...].astype(F32)
        dst = cot[r, :].astype(F32) + inv * (
            e
            - jnp.mean(e, axis=-1, keepdims=True)
            - unit * jnp.mean(e * unit, axis=-1, keepdims=True)
        )
        dstream[r, :] = dst.astype(BF)
        return carry

    lax.fori_loop(0, RD // 64, ln_back, 0)

    def spread(i, carry):
        r = rows(i * 128, 128)
        code = idx[r, :].astype(F32)
        want = (lax.broadcasted_iota(jnp.int32, (128, 128), 1) + 1).astype(F32)
        lo = jnp.where(code == want, 1.0, 0.0).astype(BF)
        hi = jnp.where(code == want + 128.0, 1.0, 0.0).astype(BF)
        back[r, :] = (mm(lo, dstream[0:128, :]) + mm(hi, dstream[128:256, :])).astype(BF)
        return carry

    lax.fori_loop(0, SLOTS // 128, spread, 0)
    for q in a3:
        q.wait_recv()
    qa = total.at[rows(c * 1024 + x * 256, 256), a_cols]
    a4 = [make(qa, qa, 18 + s, dev(z, shift(x, s), c)) for s in (1, 2, 3)]
    for q in a4:
        q.start()
    for q in b3:
        q.wait_recv()
    qb = total.at[rows(c * 1024 + z * 256, 256), b_cols]
    b4 = [make(qb, qb, 21 + s, dev(shift(z, s), x, c)) for s in (1, 2, 3)]
    for q in b4:
        q.start()
    go()
    for q in a4 + b4:
        q.wait_recv()
    half = total.at[rows(c * 1024, 1024)]
    last = make(half, half, 25, dev(z, x, other))
    last.start()
    done()

    def collect(i, carry):
        r = rows(i * 128, 128)
        col = pl.ds(pl.multiple_of(i * 128, 128), 128)
        dpatch[r, :] = mm(sel[:, col], ret[...], 0, 0).astype(BF)
        return carry

    lax.fori_loop(0, RD // 128, collect, 0)
    last.wait_recv()
    drain()
    for q in [swap, last] + a1 + b1 + a2 + b2 + a3 + b3 + a4 + b4:
        q.wait_send()


def sds(*shape):
    return jax.ShapeDtypeStruct(shape, BF)


def vm(*shape):
    return pltpu.VMEM(shape, BF)


def params(n):
    return pltpu.CompilerParams(
        collective_id=n, has_side_effects=True, vmem_limit_bytes=60 * 2**20
    )


def dma(n):
    return pltpu.SemaphoreType.DMA((n,))


def local(
    patch_rows, packing, segment, coords, pos_rows, pos_cols, norm_gain, w_qkv, w_out, cotangent
):
    total_rows = RD * lax.axis_size("dp") * lax.axis_size("mp")
    coef = jnp.full((1,), total_rows ** (-0.5), F32)
    wq = jnp.pad(
        w_qkv.reshape(D, 3, NH, HD).transpose(0, 2, 1, 3), ((0, 0), (0, 0), (0, 0), (0, HP - HD))
    ).reshape(D, NH * 3 * HP)
    wo = jnp.pad(w_out.reshape(NH, HD, D), ((0, 0), (0, HP - HD), (0, 0))).reshape(NH * HP, D)
    pos = jnp.concatenate([pos_rows, pos_cols], axis=0)
    gain = norm_gain.reshape(1, D)
    stream, ng, cotg, qkv, datt, idx, sel = pl.pallas_call(
        dispatch_kernel,
        out_shape=(
            sds(RD, D), sds(SEQ, D), sds(SEQ, D), sds(SEQ, NH * 3 * HP), sds(SEQ, NH * HP),
            sds(SLOTS, 128), sds(SLOTS, RD),
        ),
        in_specs=[VM] * 9,
        out_specs=[VM] * 7,
        scratch_shapes=[
            vm(SLOTS, D + 128), vm(SLOTS, D + 128),
            dma(NDP), dma(NDP), dma(6), dma(6), dma(6), dma(6),
        ],
        compiler_params=params(0),
        name="dispatch",
    )(patch_rows, packing.T, packing, coords.T, pos, gain, wq, wo, cotangent)
    h = RD // 2
    grad, dnp, output = pl.pallas_call(
        attention_kernel,
        out_shape=(sds(NH * 512, D), sds(SEQ, D), sds(RD, D)),
        in_specs=[pl.BlockSpec(memory_space=pltpu.SMEM)] + [VM] * 9,
        out_specs=[VM] * 3,
        scratch_shapes=[
            vm(NH, 256, 2048), vm(SEQ, NH * HP), vm(SEQ, NH * 3 * HP),
            pltpu.VMEM((SEQ, HP), F32), pltpu.VMEM((SEQ, HP), F32),
            vm(SEQ, D), vm(h, D), vm(h, D), vm(RD, D), vm(RD, D), dma(6), dma(6),
        ],
        compiler_params=params(1),
        name="attention",
    )(coef, qkv, datt, ng, cotg, segment.reshape(SEQ, 1), segment.reshape(1, SEQ), wq, wo, stream)
    total, d_patches = pl.pallas_call(
        reduce_kernel,
        out_shape=(sds(NH * 512, D), sds(RD, D)),
        in_specs=[VM] * 7,
        out_specs=[VM] * 2,
        scratch_shapes=[
            vm(SEQ, D), vm(h, D), vm(h, D), vm(RD, D), vm(RD, D),
            vm(1024, D), vm(1024, D),
            vm(3, 256, CA), vm(3, 64, CA), vm(3, 256, D - CA), vm(3, 64, D - CA),
            vm(256, CA), vm(256, D - CA), vm(SLOTS, D), vm(SLOTS, D), vm(RD, D),
            dma(6), dma(6), dma(26), dma(26), dma(NDP), dma(NDP),
        ],
        compiler_params=params(2),
        name="reduce",
    )(grad, dnp, stream, cotangent, idx, sel, gain)
    parts = total.reshape(NH, 4, HP, D)[:, :, :HD]
    grad_qkv = parts[:, :3].transpose(3, 1, 0, 2).reshape(D, 3, NH * HD).astype(F32)
    grad_out = parts[:, 3].reshape(NH * HD, D).astype(F32)
    return (output, d_patches, grad_qkv, grad_out)


def solution(mesh):
    placed = (
        P(("dp", "mp"), None),
        P(None, ("dp", "mp")),
        P("dp"),
        P(None, ("dp", "mp")),
        P(),
        P(),
        P(),
        P(None, None, "mp"),
        P("mp", None),
        P(("dp", "mp"), None),
    )
    return jax.shard_map(
        local,
        mesh=mesh,
        in_specs=placed,
        out_specs=(
            P(("dp", "mp"), None),
            P(("dp", "mp"), None),
            P(None, None, "mp"),
            P("mp", None),
        ),
        check_vma=False,
    )
```

time: 403 us -> 260 us (0.65); the launches traced: 396 us -> 260 us
  waiting for transfers between devices: 238 us -> 0 us
  Pallas kernels: 0 us -> 225 us
  matrix products: 68.9 us -> 0 us
  other arithmetic: 30.3 us -> 3.83 us
  starting transfers between devices: 22.4 us -> 0 us
  between operations: 14.5 us -> 0.7 us
  local copies, waits for them, and re-layouts: 21.5 us -> 29.9 us
    pallas_call x0 -> x3, Pallas kernels: none -> 225 us  [the longest x1 97 us: local(): pl.pallas_call(reduce_kernel, out_shape=(sds(NH * 512, D), sds(RD, D)), i...]
    psum x1 -> x0, waiting for transfers between devices: 116 us -> none  [local(): lax.psum(grad_qkv.astype(jnp.bfloat16), 'dp').astype(jnp.float32)]
    reduce_scatter x2 -> x0, waiting for transfers between devices: 62.6 us -> none  [the longest x1 40.7 us: local(): lax.psum_scatter(jnp.dot(block_rows, w_out, preferred_element_type=jnp.fl...]
    dot_general x13 -> x0, matrix products: 55.3 us -> none  [the longest x1 8.27 us: local(): lax.dot_general(gathered, d_qkv, (((0,), (0,)), ((), ())), preferred_elem...]
    all_gather x2 -> x0, waiting for transfers between devices: 33.8 us -> none  [the longest x1 33.8 us: local(): gathered = lax.all_gather(normed, 'mp', axis=0, tiled=True)]
    all_to_all x3 -> x0, waiting for transfers between devices: 24.9 us -> none  [the longest x1 22.1 us: local(): lax.all_to_all(send_rows, 'dp', split_axis=0, concat_axis=0, tiled=True)]
    all_to_all x3 -> x0, starting transfers between devices: 21.7 us -> none  [the longest x1 9.43 us: local(): lax.all_to_all(send_index, 'dp', split_axis=0, concat_axis=0, tiled=True)]
    convert_element_type x7 -> x2, other arithmetic: 19.3 us -> 2.36 us  [the longest x1 1.82 us: local(): grad_out = parts[:, 3].reshape(NH * HD, D).astype(F32)]
  transfers between devices with their start and end apart: 8 -> 0, of which waited for: 6 -> 0; matrix products, arithmetic and copies ran while one was open for 15% -> 0% of each run, Pallas kernels for 0% -> 0%
where the time goes in v1:
time: 260 us
  Pallas kernels  225 us (87%)
  local copies, waits for them, and re-layouts  29.9 us (12%)
  other arithmetic  3.83 us (1%)
    pallas_call x1, Pallas kernels, local(): pl.pallas_call(reduce_kernel, out_shape=(sds(NH * 512, D), sds(RD, D)), i...  97 us
    pallas_call x1, Pallas kernels, local(): pl.pallas_call(dispatch_kernel, out_shape=(sds(RD, D), sds(SEQ, D), sds(S...  79.3 us
    pallas_call x1, Pallas kernels, local(): pl.pallas_call(attention_kernel, out_shape=(sds(NH * 512, D), sds(SEQ, D)...  48.8 us
    unnamed x11, local copies, waits for them, and re-layouts  8.17 us
    reshape x1, local copies, waits for them, and re-layouts, local(): wq = jnp.pad(w_qkv.reshape(D, 3, NH, HD).transpose(0, 2, 1, 3), ((0, 0),...  7.76 us

profile of v1, /device:TPU:1, one launch (start us, length us, event | category | flops | bytes accessed | tf_op | source)
XLA Modules:
  0.0 259.6 jit_solution(12054042654856136283)
XLA Ops:
  0.6 1.3 reshape.37.gain
  1.9 1.5 pad_maximum_fusion.pos
  3.4 1.5 copy.25
  4.9 1.5 copy.24
  6.4 1.7 copy.28.seg_col
  8.1 2.6 %pad.9 = bf16[4,128,1664]{2,1,0:T(8,128)(2,1)} pad(bf16[4,104,1664]{2,1,0:T(8,128)(2,1)} %bitcast.24, bf16[]{:T(256)} %constant.4.clone.1), padding=0_0x0_24x0_0 | pad | bytes 3088386 | tf_op jit(solution)/shard_map/jit(_pad)/pad | solution.py:539
  10.7 2.5 copy.31
  13.2 2.8 %pad.8.clone = bf16[1664,4,3,128]{0,3,2,1:T(8,128)(2,1)} pad(bf16[1664,4,3,104]{0,3,2,1:T(8,128)(2,1)S(1)} %copy.31, bf16[]{:T(256)} %constant.4.clone.1), padding=0_0x0_0x0_0x0_24 | pad | bytes 9265154 | tf_op jit(solution)/shard_map/jit(_pad)/pad | solution.py:536
  16.0 7.8 %copy.27.wq = bf16[1664,1536]{1,0:T(8,128)(2,1)} copy(bf16[1664,1536]{0,1:T(8,128)(2,1)} %bitcast.17) | data formatting | bytes 10223616 | tf_op jit(solution)/shard_map/reshape | solution.py:538
  23.8 79.3 %dispatch.1 = (bf16[256,1664]{1,0:T(8,128)(2,1)}, bf16[1024,1664]{1,0:T(8,128)(2,1)}, bf16[1024,1664]{1,0:T(8,128)(2,1)}, bf16[1024,1536]{1,0:T(8,128)(2,1)}, bf...) custom-call(bf16[256,1664]{1,0:T(8,128)(2,1)} %patch.1, s32[256,2]{1,0:T(8,128)} %bitcast.26, ...), custom_call_target="tpu_custom_call" | custom-call | tf_op jit(solution)/shard_map/dispatch/pallas_call | solution.py:542
  103.1 48.8 %attention.1 = (bf16[2048,1664]{1,0:T(8,128)(2,1)}, bf16[1024,1664]{1,0:T(8,128)(2,1)}, bf16[256,1664]{1,0:T(8,128)(2,1)}) custom-call(f32[1]{0:T(128)} %constant.1.clone.1.scal, bf16[1024,1536]{1,0:T(8,128)(2,1)} %get-tuple-element.16.qkv, bf16[1024,512]{1,0:T(8,128)(2,1)} %get-tuple-element.17.datt, bf16[1024,1664]{1,0:T(8,128)(2,1)} %get-tuple-element.18.ng, ...), custom_call_target="tpu_custom_call" | custom-call | tf_op jit(solution)/shard_map/attention/pallas_call | solution.py:558
  151.9 97.0 %reduce.1 = (bf16[2048,1664]{1,0:T(8,128)(2,1)}, bf16[256,1664]{1,0:T(8,128)(2,1)}) custom-call(bf16[2048,1664]{1,0:T(8,128)(2,1)} %get-tuple-element.22.grad, bf16[1024,1664]{1,0:T(8,128)(2,1)} %get-tuple-element.23.dnp_in, bf16[256,1664]{1,0:T(8,128)(2,1)} %get-tuple-element.20.stream, bf16[256,1664]{1,0:T(8,128)(2,1)} %cot.3, ...), custom_call_target="tpu_custom_call" | custom-call | tf_op jit(solution)/shard_map/reduce/pallas_call | solution.py:571
  248.9 0.0 copy-start
  248.9 1.6 slice.12
  250.5 1.8 bitcast_convert_fusion
  252.4 0.9 copy-done
  253.3 0.5 convert_bitcast_fusion
  253.8 0.0 copy-start.1
  253.8 0.0 copy-start.2
  253.8 3.9 %copy.30 = f32[1664,3,4,104]{0,3,2,1:T(8,128)} copy(f32[1664,3,4,104]{0,3,1,2:T(8,128)S(1)} %convert_bitcast_fusion) | data formatting | bytes 16613376 | tf_op jit(solution)/shard_map/convert_element_type | solution.py:587
  257.8 0.0 copy-done.1
  257.8 0.9 copy.34
  258.7 0.0 copy-done.2
  258.7 0.9 copy.35
Async XLA Ops:
  248.9 4.4 %copy-start = (bf16[2048,1664]{1,0:T(8,128)(2,1)S(1)}, bf16[2048,1664]{1,0:T(8,128)(2,1)}, u32[]{:S(2)}) copy-start(bf16[2048,1664]{1,0:T(8,128)(2,1)} %get-tuple-element.27) | copy-start | bytes 20447236
  253.8 4.0 %copy-start.1 = (bf16[256,1664]{1,0:T(8,128)(2,1)S(1)}, bf16[256,1664]{1,0:T(8,128)(2,1)}, u32[]{:S(2)}) copy-start(bf16[256,1664]{1,0:T(8,128)(2,1)} %get-tuple-element.32) | copy-start | bytes 2555908
  253.8 4.8 %copy-start.2 = (bf16[256,1664]{1,0:T(8,128)(2,1)S(1)}, bf16[256,1664]{1,0:T(8,128)(2,1)}, u32[]{:S(2)}) copy-start(bf16[256,1664]{1,0:T(8,128)(2,1)} %get-tuple-element.33) | copy-start | bytes 2555908

commit v2 on v1

v2 whole, which is shorter than its diff:
```python
import jax
import jax.numpy as jnp
from jax import lax
from jax.experimental import pallas as pl
from jax.experimental.pallas import tpu as pltpu
from jax.sharding import PartitionSpec as P

HD = 104
HP = 128
NH = 4
D = 1664
RD = 256
SEQ = 1024
CAP = 16
NDP = 32
SLOTS = NDP * CAP
CA = 896
GW = NH * HD
MESH = pl.DeviceIdType.MESH
F32 = jnp.float32
BF = jnp.bfloat16
VM = pl.BlockSpec(memory_space=pltpu.VMEM)
BLOCKS = ((0, 0, 256, 0), (256, 256, 768, 256), (512, 256, 1024, 768), (768, 512, 1024, 1536))


def mm(a, b, ca=1, cb=0):
    return lax.dot_general(a, b, (((ca,), (cb,)), ((), ())), preferred_element_type=F32)


def rows(start, size):
    return pl.ds(pl.multiple_of(start, 16), size)


def place():
    dp, mp = lax.axis_index("dp"), lax.axis_index("mp")
    return dp, mp, lax.rem(mp + 1, 4), lax.rem(mp + 3, 4), lax.rem(mp + 2, 4)


def copier(ssem, rsem):
    def make(src, dst, n, dev):
        return pltpu.make_async_remote_copy(
            src, dst, ssem.at[n], rsem.at[n], device_id=dev, device_id_type=MESH
        )

    return make


def greet(devs):
    bar = pltpu.get_barrier_semaphore()
    for dev in devs:
        pl.semaphore_signal(bar, inc=1, device_id=dev, device_id_type=MESH)
    return bar


def greet_dp(dp, mp, right, left):
    bar = greet(((dp, right), (dp, left)))

    def one(i, carry):
        pl.semaphore_signal(
            bar, inc=1, device_id=(lax.rem(dp + i, NDP), mp), device_id_type=MESH
        )
        return carry

    lax.fori_loop(1, NDP, one, 0)
    return bar


def a2a_copies(src, dst, ssem, rsem, dp, mp, width=D + 128):
    def make(i):
        d = lax.rem(dp + i, NDP)
        return pltpu.make_async_remote_copy(
            src.at[rows(d * CAP, CAP), 0:width],
            dst.at[rows(dp * CAP, CAP), 0:width],
            ssem.at[i],
            rsem.at[i],
            device_id=(d, mp),
            device_id_type=MESH,
        )

    def start():
        def one(i, carry):
            make(i).start()
            return carry

        lax.fori_loop(1, NDP, one, 0)
        dst[rows(dp * CAP, CAP), 0:width] = src[rows(dp * CAP, CAP), 0:width]

    def wait():
        def one(i, carry):
            make(i).wait()
            return carry

        lax.fori_loop(1, NDP, one, 0)

    return start, wait


def ring_gather(src, dst, ssem, rsem, dp, mp, right, left):
    make = copier(ssem, rsem)
    h = RD // 2

    def at(dev, half):
        return dst.at[rows(dev * RD + half * h, h)]

    a0 = make(src.at[0:h], at(mp, 0), 0, (dp, right))
    b1 = make(src.at[h:RD], at(mp, 1), 1, (dp, left))
    a1 = make(src.at[h:RD], at(mp, 1), 2, (dp, right))
    b0 = make(src.at[0:h], at(mp, 0), 3, (dp, left))
    f0 = make(at(left, 0), at(left, 0), 4, (dp, right))
    f1 = make(at(right, 1), at(right, 1), 5, (dp, left))

    def start():
        for c in (a0, b1, a1, b0):
            c.start()

    def onward():
        a0.wait_recv()
        f0.start()
        b1.wait_recv()
        f1.start()

    def near():
        a1.wait_recv()
        b0.wait_recv()

    def far():
        f0.wait_recv()
        f1.wait_recv()

    def drain():
        for c in (a0, b1, a1, b0, f0, f1):
            c.wait_send()

    return start, onward, near, far, drain


def ring_reduce(part, ha, hb, fl, fr, ssem, rsem, dp, mp, right, left, opp):
    make = copier(ssem, rsem)
    h = RD // 2

    def at(dev, half):
        return part.at[rows(dev * RD + half * h, h)]

    s0 = make(at(opp, 0), ha, 0, (dp, right))
    s1 = make(at(opp, 1), hb, 1, (dp, left))
    s2 = make(at(right, 1), fl.at[h:RD], 2, (dp, right))
    s3 = make(at(left, 0), fr.at[0:h], 3, (dp, left))
    s4 = make(at(right, 0), fl.at[0:h], 4, (dp, right))
    s5 = make(at(left, 1), fr.at[h:RD], 5, (dp, left))

    def first():
        s0.start()
        s1.start()

    def second():
        s2.start()
        s3.start()

    def onward():
        s0.wait_recv()
        r0 = rows(right * RD, h)
        part[r0] = (part[r0].astype(F32) + ha[...].astype(F32)).astype(BF)
        s4.start()
        s1.wait_recv()
        r1 = rows(left * RD + h, h)
        part[r1] = (part[r1].astype(F32) + hb[...].astype(F32)).astype(BF)
        s5.start()

    def finish():
        for c in (s2, s3, s4, s5):
            c.wait_recv()

    def drain():
        for c in (s0, s1, s2, s3, s4, s5):
            c.wait_send()

    return first, second, onward, finish, drain


def column(row):
    n = row.shape[1]
    eye = lax.broadcasted_iota(jnp.int32, (n, n), 0) == lax.broadcasted_iota(jnp.int32, (n, n), 1)
    return jnp.sum(jnp.where(eye, row.astype(F32), 0.0), axis=1, keepdims=True).astype(jnp.int32)


def layer_norm(stream_rows):
    sf = stream_rows.astype(F32)
    cen = sf - jnp.mean(sf, axis=-1, keepdims=True)
    inv = lax.rsqrt(jnp.mean(cen * cen, axis=-1, keepdims=True) + 1e-06)
    return cen * inv, inv


def head_cols(h):
    base = h * 3 * HP
    return [pl.ds(pl.multiple_of(base + k * HP, 128), HP) for k in range(3)]


def sublayer_kernel(
    packing, coords, seg, prow, pcol, gain, patch_in, w_in, wo_in, cot_in,
    out, dpatch, total,
    stream, ng, cotg, qkv, datt, idx, sel, wq, wo, crd, segc,
    send, recv, ret, prob, att, dk, dv, part, dnp, grad,
    ha, hb, fl, fr, ha2, hb2, fl2, fr2, core_in, ax, az, bx, bz,
    as_, ar, bs, br, cs, cr, ns, nr, os_, or_, ys, yr, gs, gr, ls, lk,
):
    dp, mp, right, left, opp = place()
    c = lax.rem(dp, 2)
    x = lax.rem(dp // 2, 4)
    z = dp // 8
    other = 1 - c
    scale = HD ** (-0.5)
    coef = (RD * NDP * 4) ** (-0.5)
    bar = greet_dp(dp, mp, right, left)
    l_w = pltpu.make_async_copy(w_in, grad.at[0:3, 0:GW], ls.at[0])
    l_o = pltpu.make_async_copy(wo_in, grad.at[3, 0:GW], ls.at[1])
    l_c = pltpu.make_async_copy(cot_in, cotg.at[rows(mp * RD, RD)], ls.at[2])
    patch = part.at[0:RD]
    l_p = pltpu.make_async_copy(patch_in, patch, ls.at[7])
    l_p.start()
    l_c.start()
    l_w.start()
    l_o.start()

    g_row = packing[0:1, :]
    src_i = lax.broadcasted_iota(jnp.int32, (RD, RD), 0)
    dst_i = lax.broadcasted_iota(jnp.int32, (RD, RD), 1)
    before = jnp.where((column(g_row) == g_row) & (src_i < dst_i), 1.0, 0.0)
    rank = jnp.sum(before, axis=0, keepdims=True).astype(jnp.int32)
    placed = g_row * CAP + rank
    ext = jnp.broadcast_to((column(packing[1:2, :]) + 1).astype(F32), (RD, 128)).astype(BF)

    l_p.wait()

    def fill(i, carry):
        at = rows(i * 128, 128)
        slot = lax.broadcasted_iota(jnp.int32, (128, RD), 0) + i * 128
        pick = jnp.where(slot == placed, 1.0, 0.0).astype(BF)
        sel[at, :] = pick
        send[at, 0:D] = mm(pick, patch[...]).astype(BF)
        send[at, D:] = mm(pick, ext).astype(BF)
        return carry

    lax.fori_loop(0, SLOTS // 128, fill, 0)
    pl.semaphore_wait(bar, NDP + 1)
    go, done = a2a_copies(send, recv, as_, ar, dp, mp)
    go()
    l_c.wait()
    c_start, c_onward, c_near, c_far, c_drain = ring_gather(
        cotg.at[rows(mp * RD, RD)], cotg, cs, cr, dp, mp, right, left
    )
    c_start()

    crd[:, 0:1] = column(coords[0:1, :])
    crd[:, 1:2] = column(coords[1:2, :])
    for i in range(4):
        segc[i * 256 : (i + 1) * 256, :] = column(seg[:, i * 256 : (i + 1) * 256])
    l_w.wait()
    l_o.wait()

    def pad_head(h, carry):
        i0 = lax.broadcasted_iota(jnp.int32, (HP, GW), 0)
        i1 = lax.broadcasted_iota(jnp.int32, (HP, GW), 1)
        pick = jnp.where((i1 == i0 + h * HD) & (i0 < HD), 1.0, 0.0).astype(BF)

        def one(k, inner):
            wq[rows(h * 3 * HP + k * HP, HP), :] = mm(pick, grad[k, 0:GW, :]).astype(BF)
            return inner

        lax.fori_loop(0, 3, one, 0)
        wo[rows(h * HP, HP), :] = mm(pick, grad[3, 0:GW, :]).astype(BF)
        return carry

    lax.fori_loop(0, NH, pad_head, 0)
    c_onward()
    done()
    idx[...] = recv[:, D:]

    def unpack(i, carry):
        at = rows(i * 128, 128)
        code = recv[:, D:].astype(F32)
        want = (lax.broadcasted_iota(jnp.int32, (SLOTS, 128), 1) + (i * 128 + 1)).astype(F32)
        pick = jnp.where(code == want, 1.0, 0.0).astype(BF)
        packed = mm(pick, recv[:, 0:D], 0, 0)
        gi = lax.broadcasted_iota(jnp.int32, (128, 16), 1)
        row_hot = jnp.where(gi == crd[at, 0:1], 1.0, 0.0).astype(BF)
        col_hot = jnp.where(gi == crd[at, 1:2], 1.0, 0.0).astype(BF)
        s = (packed + mm(row_hot, prow[...]) + mm(col_hot, pcol[...])).astype(BF)
        stream[at, :] = s
        unit, _ = layer_norm(s)
        ng[rows(mp * RD + i * 128, 128), :] = (unit * gain[...].astype(F32)).astype(BF)
        return carry

    lax.fori_loop(0, RD // 128, unpack, 0)
    n_start, n_onward, n_near, n_far, n_drain = ring_gather(
        ng.at[rows(mp * RD, RD)], ng, ns, nr, dp, mp, right, left
    )
    n_start()

    def project(s):
        def one(n, carry):
            col = pl.ds(pl.multiple_of(n * 512, 128), 512)
            qkv[rows(s * RD, RD), col] = mm(
                ng[rows(s * RD, RD)], wq[rows(n * 512, 512), :], 1, 1
            ).astype(BF)
            return carry

        lax.fori_loop(0, 3, one, 0)

    def back_project(s):
        datt[rows(s * RD, RD), :] = mm(cotg[rows(s * RD, RD)], wo[...], 1, 1).astype(BF)

    project(mp)
    back_project(mp)
    c_near()
    c_far()
    back_project(right)
    back_project(left)
    back_project(opp)
    n_onward()
    n_near()
    project(right)
    project(left)
    n_far()
    project(opp)

    def fwd(h, carry):
        qc, kc, vc = head_cols(h)
        hc = pl.ds(pl.multiple_of(h * HP, 128), HP)
        for r0, k0, k1, p0 in BLOCKS:
            s = mm(qkv[r0 : r0 + 256, qc], qkv[k0:k1, kc], 1, 1) * scale
            same = segc[r0 : r0 + 256, :] == seg[:, k0:k1]
            s = jnp.where(same, s, -1e30)
            e = jnp.where(same, jnp.exp(s - jnp.max(s, axis=-1, keepdims=True)), 0.0)
            p = (e / jnp.sum(e, axis=-1, keepdims=True)).astype(BF)
            prob[h, :, p0 : p0 + k1 - k0] = p
            att[r0 : r0 + 256, hc] = mm(p, qkv[k0:k1, vc]).astype(BF)
        return carry

    lax.fori_loop(0, NH, fwd, 0)
    first, second, onward, finish, drain = ring_reduce(
        part, ha, hb, fl, fr, os_, or_, dp, mp, right, left, opp
    )

    def out_rows(s):
        part[rows(s * RD, RD), :] = mm(att[rows(s * RD, RD), :], wo[...]).astype(BF)

    out_rows(opp)
    first()
    out_rows(right)
    out_rows(left)
    second()
    out_rows(mp)

    def dev(zz, xx, cc):
        return ((zz * 4 + xx) * 2 + cc, mp)

    def shift(v, s):
        return lax.rem(v + s, 4)

    halves = (pl.ds(0, CA), pl.ds(CA, D - CA))

    def piece(h, r, size, cols):
        return grad.at[2 * c + r // HP, rows(h * HP + lax.rem(r, HP), size), cols]

    def placed_piece(h, r, size, cols):
        return total.at[2 * c + r // HP, rows(h * HP + lax.rem(r, HP), size), cols]

    class Stage:
        def __init__(self, h):
            def make(src, dst, n, to):
                return pltpu.make_async_remote_copy(
                    src, dst, gs.at[h, n], gr.at[h, n], device_id=to, device_id_type=MESH
                )

            def far(axis, s):
                return dev(z, shift(x, s), c) if axis == 0 else dev(shift(z, s), x, c)

            self.h = h
            self.make, self.far = make, far

        def swap(self):
            hr = rows(self.h * HP, HP)
            return self.make(
                grad.at[pl.ds(2 * other, 2), hr], core_in.at[self.h], 0, dev(z, x, other)
            )

        def last(self):
            ours = total.at[pl.ds(2 * c, 2), rows(self.h * HP, HP)]
            return self.make(ours, ours, 25, dev(z, x, other))

        def group(self, kind, a):
            one, two = (x, z) if a == 0 else (z, x)
            copies = []
            for s in (1, 2, 3):
                if kind == 0:
                    src = piece(self.h, shift(one, s) * 64, 64, halves[a])
                    dst = (ax, bx)[a].at[self.h, s - 1]
                elif kind == 1:
                    src = piece(self.h, one * 64 + shift(two, s) * 16, 16, halves[a])
                    dst = (az, bz)[a].at[self.h, s - 1]
                elif kind == 2:
                    src = piece(self.h, one * 64 + two * 16, 16, halves[a])
                    dst = placed_piece(self.h, one * 64 + two * 16, 16, halves[a])
                else:
                    src = dst = placed_piece(self.h, one * 64, 64, halves[a])
                axis = a if kind in (0, 3) else 1 - a
                copies.append(self.make(src, dst, 12 * a + 3 * kind + s, self.far(axis, s)))
            return copies

        def keep(self, a):
            one, two = (x, z) if a == 0 else (z, x)
            r = one * 64 + two * 16
            return pltpu.make_async_copy(
                piece(self.h, r, 16, halves[a]),
                placed_piece(self.h, r, 16, halves[a]),
                lk.at[self.h, a],
            )

        def s0(self):
            self.swap().start()

        def s1(self):
            h = self.h
            self.swap().wait_recv()
            hr = rows(h * HP, HP)
            for k in range(2):
                mine = grad[2 * c + k, hr, :].astype(F32)
                grad[2 * c + k, hr, :] = (mine + core_in[h, k].astype(F32)).astype(BF)
            big = self.group(0, 0), self.group(0, 1)
            for s in (1, 0, 2):
                for a in range(2):
                    big[a][s].start()

        def gather(self, copies, ref, incoming, nxt):
            for q in copies:
                q.wait_recv()
            val = ref[...].astype(F32)
            for s in range(3):
                val += incoming[self.h, s].astype(F32)
            ref[...] = val.astype(BF)
            for q in nxt:
                q.start()

        def s2(self):
            for a, b_in in enumerate((ax, bx)):
                one = x if a == 0 else z
                ref = piece(self.h, one * 64, 64, halves[a])
                self.gather(self.group(0, a), ref, b_in, self.group(1, a))

        def s3(self):
            for a, s_in in enumerate((az, bz)):
                one, two = (x, z) if a == 0 else (z, x)
                ref = piece(self.h, one * 64 + two * 16, 16, halves[a])
                self.gather(self.group(1, a), ref, s_in, self.group(2, a) + [self.keep(a)])

        def s4(self):
            for a in range(2):
                self.keep(a).wait()
                for q in self.group(2, a):
                    q.wait_recv()
                for q in self.group(3, a):
                    q.start()

        def s5(self):
            for a in range(2):
                for q in self.group(3, a):
                    q.wait_recv()
            self.last().start()

        def s6(self):
            self.last().wait_recv()

        def s7(self):
            sent = [self.swap(), self.last()]
            for kind in range(4):
                sent += self.group(kind, 0) + self.group(kind, 1)
            for q in sent:
                q.wait_send()

    def weight_grad(h):
        hr = rows(h * HP, HP)
        all3 = pl.ds(pl.multiple_of(h * 3 * HP, 128), 3 * HP)
        g = (mm(qkv[:, all3], ng[...], 0, 0) * coef).astype(BF)
        for k in range(3):
            grad[k, hr, :] = g[k * HP : (k + 1) * HP]
        hc = pl.ds(pl.multiple_of(h * HP, 128), HP)
        grad[3, hr, :] = (mm(att[:, hc], cotg[...], 0, 0) * coef).astype(BF)
        Stage(h).s0()

    def bwd(h, carry):
        qc, kc, vc = head_cols(h)
        hc = pl.ds(pl.multiple_of(h * HP, 128), HP)
        dk[...] = jnp.zeros_like(dk)
        dv[...] = jnp.zeros_like(dv)
        for r0, k0, k1, p0 in BLOCKS:
            p = prob[h, :, p0 : p0 + k1 - k0]
            da = datt[r0 : r0 + 256, hc]
            delta = jnp.sum(
                da.astype(F32) * att[r0 : r0 + 256, hc].astype(F32), axis=-1, keepdims=True
            )
            dprob = mm(da, qkv[k0:k1, vc], 1, 1)
            ds = (p.astype(F32) * (dprob - delta) * scale).astype(BF)
            dk[k0:k1, :] += mm(ds, qkv[r0 : r0 + 256, qc], 0, 0)
            dv[k0:k1, :] += mm(p, da, 0, 0)
            qkv[r0 : r0 + 256, qc] = mm(ds, qkv[k0:k1, kc]).astype(BF)
        qkv[:, kc] = dk[...].astype(BF)
        qkv[:, vc] = dv[...].astype(BF)

        @pl.when(h >= 1)
        def _():
            weight_grad(h - 1)

        @pl.when(h >= 2)
        def _():
            Stage(h - 2).s1()

        @pl.when(h == 1)
        def _():
            onward()

        @pl.when(h == 3)
        def _():
            Stage(h - 3).s2()

        return carry

    lax.fori_loop(0, NH, bwd, 0)
    first2, second2, onward2, finish2, drain2 = ring_reduce(
        dnp, ha2, hb2, fl2, fr2, ys, yr, dp, mp, right, left, opp
    )

    def d_rows(s):
        dnp[rows(s * RD, RD), :] = mm(qkv[rows(s * RD, RD), :], wq[...]).astype(BF)

    d_rows(opp)
    first2()
    d_rows(right)
    d_rows(left)
    second2()
    weight_grad(3)
    d_rows(mp)
    st = [Stage(h) for h in range(NH)]
    st[2].s1()
    onward2()
    st[1].s2()
    st[0].s3()
    st[3].s1()
    finish()
    acc = part[rows(mp * RD, RD)].astype(F32) + fl[...].astype(F32) + fr[...].astype(F32)
    part[rows(mp * RD, RD)] = (stream[...].astype(F32) + acc).astype(BF)
    l_out = pltpu.make_async_copy(part.at[rows(mp * RD, RD)], out, ls.at[8])
    l_out.start()
    st[2].s2()
    st[1].s3()
    st[0].s4()
    st[3].s2()
    st[2].s3()
    st[1].s4()
    st[0].s5()
    finish2()
    back = send
    go_back, done_back = a2a_copies(back, ret, bs, br, dp, mp, D)

    def ln_back(i, carry):
        r = rows(i * 64, 64)
        unit, inv = layer_norm(stream[r, :])
        dn = dnp[rows(mp * RD + i * 64, 64), :].astype(F32)
        e = (dn + fl2[r, :].astype(F32) + fr2[r, :].astype(F32)) * gain[...].astype(F32)
        dst = cotg[rows(mp * RD + i * 64, 64), :].astype(F32) + inv * (
            e
            - jnp.mean(e, axis=-1, keepdims=True)
            - unit * jnp.mean(e * unit, axis=-1, keepdims=True)
        )
        stream[r, :] = dst.astype(BF)
        return carry

    lax.fori_loop(0, RD // 64, ln_back, 0)

    def spread(i, carry):
        r = rows(i * 128, 128)
        code = idx[r, :].astype(F32)
        want = (lax.broadcasted_iota(jnp.int32, (128, 128), 1) + 1).astype(F32)
        lo = jnp.where(code == want, 1.0, 0.0).astype(BF)
        hi = jnp.where(code == want + 128.0, 1.0, 0.0).astype(BF)
        back[r, 0:D] = (mm(lo, stream[0:128, :]) + mm(hi, stream[128:256, :])).astype(BF)
        return carry

    lax.fori_loop(0, SLOTS // 128, spread, 0)
    go_back()
    st[3].s3()
    st[2].s4()
    st[1].s5()
    st[0].s6()
    st[3].s4()
    st[2].s5()
    st[1].s6()
    st[3].s5()
    st[2].s6()
    done_back()

    def collect(i, carry):
        r = rows(i * 128, 128)
        col = pl.ds(pl.multiple_of(i * 128, 128), 128)
        recv[r, 0:D] = mm(sel[:, col], ret[...], 0, 0).astype(BF)
        return carry

    lax.fori_loop(0, RD // 128, collect, 0)
    l_dp = pltpu.make_async_copy(recv.at[0:RD, 0:D], dpatch, ls.at[9])
    l_dp.start()
    st[3].s6()

    def settle(h, carry):
        Stage(h).s7()
        return carry

    lax.fori_loop(0, NH, settle, 0)
    c_drain()
    n_drain()
    drain()
    drain2()
    l_out.wait()
    l_dp.wait()


def sds(*shape):
    return jax.ShapeDtypeStruct(shape, BF)


def vm(*shape):
    return pltpu.VMEM(shape, BF)


def dma(*n):
    return pltpu.SemaphoreType.DMA(n)


def local(
    patch_rows, packing, segment, coords, pos_rows, pos_cols, norm_gain, w_qkv, w_out, cotangent
):
    h = RD // 2
    anywhere = pl.BlockSpec(memory_space=pl.ANY)
    output, d_patches, total = pl.pallas_call(
        sublayer_kernel,
        out_shape=(sds(RD, D), sds(RD, D), sds(4, NH * HP, D)),
        in_specs=[VM] * 6 + [anywhere] * 4,
        out_specs=[anywhere] * 3,
        scratch_shapes=[
            vm(RD, D), vm(SEQ, D), vm(SEQ, D), vm(SEQ, NH * 3 * HP), vm(SEQ, NH * HP),
            vm(SLOTS, 128), vm(SLOTS, RD), vm(NH * 3 * HP, D), vm(NH * HP, D),
            pltpu.VMEM((RD, 2), jnp.int32), pltpu.VMEM((SEQ, 1), jnp.int32),
            vm(SLOTS, D + 128), vm(SLOTS, D + 128), vm(SLOTS, D),
            vm(NH, 256, 2048), vm(SEQ, NH * HP),
            pltpu.VMEM((SEQ, HP), F32), pltpu.VMEM((SEQ, HP), F32),
            vm(SEQ, D), vm(SEQ, D), vm(4, NH * HP, D),
            vm(h, D), vm(h, D), vm(RD, D), vm(RD, D),
            vm(h, D), vm(h, D), vm(RD, D), vm(RD, D),
            vm(NH, 2, HP, D),
            vm(NH, 3, 64, CA), vm(NH, 3, 16, CA), vm(NH, 3, 64, D - CA), vm(NH, 3, 16, D - CA),
            dma(NDP), dma(NDP), dma(NDP), dma(NDP), dma(6), dma(6), dma(6), dma(6),
            dma(6), dma(6), dma(6), dma(6), dma(NH, 26), dma(NH, 26), dma(10), dma(NH, 2),
        ],
        compiler_params=pltpu.CompilerParams(
            collective_id=0, has_side_effects=True, vmem_limit_bytes=60 * 2**20
        ),
        name="sublayer",
    )(
        packing, coords, segment.reshape(1, SEQ), pos_rows, pos_cols,
        norm_gain.reshape(1, D), patch_rows, w_qkv.transpose(1, 2, 0), w_out, cotangent,
    )
    wide = total.reshape(4, NH, HP, D).astype(F32)
    grad_qkv = wide[:3, :, :HD].reshape(3, GW, D).transpose(2, 0, 1)
    grad_out = wide[3, :, :HD].reshape(GW, D)
    return (output, d_patches, grad_qkv, grad_out)


def solution(mesh):
    placed = (
        P(("dp", "mp"), None),
        P(None, ("dp", "mp")),
        P("dp"),
        P(None, ("dp", "mp")),
        P(),
        P(),
        P(),
        P(None, None, "mp"),
        P("mp", None),
        P(("dp", "mp"), None),
    )
    return jax.shard_map(
        local,
        mesh=mesh,
        in_specs=placed,
        out_specs=(
            P(("dp", "mp"), None),
            P(("dp", "mp"), None),
            P(None, None, "mp"),
            P("mp", None),
        ),
        check_vma=False,
    )
```

time: 260 us -> 191 us (0.73)
  Pallas kernels: 225 us -> 178 us
  local copies, waits for them, and re-layouts: 29.9 us -> 12.4 us
  other arithmetic: 3.83 us -> 0 us
    pallas_call x3 -> x1, Pallas kernels: 225 us -> 178 us  [local(): pl.pallas_call(sublayer_kernel, out_shape=(sds(RD, D), sds(RD, D), sds(4,...]
    reshape x3 -> x1, local copies, waits for them, and re-layouts: 10.8 us -> 1.29 us  [local(): norm_gain.reshape(1, D)]
    slice x1 -> x2, local copies, waits for them, and re-layouts: 1.6 us -> 9.27 us  [the longest x1 6.2 us: local(): grad_qkv = wide[:3, :, :HD].reshape(3, GW, D).transpose(2, 0, 1)]
    unnamed x11 -> x6, local copies, waits for them, and re-layouts: 8.17 us -> 1.81 us
    pad x2 -> x0, local copies, waits for them, and re-layouts: 5.46 us -> none  [the longest x1 2.81 us: local(): jnp.pad(w_qkv.reshape(D, 3, NH, HD).transpose(0, 2, 1, 3), ((0, 0), (0, 0...]
    convert_element_type x1 -> x0, local copies, waits for them, and re-layouts: 3.93 us -> none  [local(): parts[:, :3].transpose(3, 1, 0, 2).reshape(D, 3, NH * HD).astype(F32)]
where the time goes in v2:
time: 191 us
  Pallas kernels  178 us (93%)
  local copies, waits for them, and re-layouts  12.4 us (6%)
    pallas_call x1, Pallas kernels, local(): pl.pallas_call(sublayer_kernel, out_shape=(sds(RD, D), sds(RD, D), sds(4,...  178 us
    slice x1, local copies, waits for them, and re-layouts, local(): grad_qkv = wide[:3, :, :HD].reshape(3, GW, D).transpose(2, 0, 1)  6.2 us

profile of v2, /device:TPU:1, one launch (start us, length us, event | category | flops | bytes accessed | tf_op | source)
XLA Modules:
  0.0 190.9 jit_solution(11745299830385009487)
XLA Ops:
  0.6 1.3 reshape.21.gain
  1.9 177.9 %sublayer.1 = (bf16[256,1664]{1,0:T(8,128)(2,1)}, bf16[256,1664]{1,0:T(8,128)(2,1)}, bf16[4,512,1664]{2,1,0:T(8,128)(2,1)}) custom-call(s32[2,256]{1,0:T(2,128)} %packing.1, s32[2,256]{1,0:T(2,128)} %coords.1, s32[1,1024]{1,0:T(1,128)} %bitcast.13, bf16[16,1664]{1,0:T(8,128)(2,1)} %prow.1, bf16[16,1664]{1,0:T(8,128)(2,1)} %pcol.1, ...), custom_call_target="tpu_custom_call" | custom-call | tf_op jit(solution)/shard_map/sublayer/pallas_call | solution.py:642
  179.8 3.1 %slice.9 = f32[1,4,104,1664]{3,2,1,0:T(8,128)} slice(bf16[4,4,128,1664]{3,2,1,0:T(8,128)(2,1)} %bitcast.8), slice={[3:4], [0:4], [0:104], [0:1664]} | slice | bytes 5537792 | tf_op jit(solution)/shard_map/slice | solution.py:672
  182.9 0.0 copy-start.1
  182.9 0.0 copy-start
  182.9 6.2 %slice.8 = f32[3,4,104,1664]{3,2,1,0:T(8,128)} slice(bf16[4,4,128,1664]{3,2,1,0:T(8,128)(2,1)} %bitcast.9), slice={[0:3], [0:4], [0:104], [0:1664]} | slice | bytes 16613376 | tf_op jit(solution)/shard_map/slice | solution.py:671
  189.1 0.0 copy-done.1
  189.1 0.9 copy.16
  190.0 0.0 copy-done
  190.0 0.9 copy.17
Async XLA Ops:
  182.9 6.2 %copy-start.1 = (bf16[256,1664]{1,0:T(8,128)(2,1)S(1)}, bf16[256,1664]{1,0:T(8,128)(2,1)}, u32[]{:S(2)}) copy-start(bf16[256,1664]{1,0:T(8,128)(2,1)} %get-tuple-element.14) | copy-start | bytes 2555908
  182.9 7.1 %copy-start = (bf16[256,1664]{1,0:T(8,128)(2,1)S(1)}, bf16[256,1664]{1,0:T(8,128)(2,1)}, u32[]{:S(2)}) copy-start(bf16[256,1664]{1,0:T(8,128)(2,1)} %get-tuple-element.15) | copy-start | bytes 2555908

commit v3 on v2

--- a/solution.py
+++ b/solution.py
@@ -65,14 +65,16 @@
     return bar
 
 
-def a2a_copies(src, dst, ssem, rsem, dp, mp, width=D + 128):
+def a2a_copies(src, dst, ssem, rsem, dp, mp, first_col=0, width=D + 128, base=0):
+    cols = pl.ds(first_col, width)
+
     def make(i):
         d = lax.rem(dp + i, NDP)
         return pltpu.make_async_remote_copy(
-            src.at[rows(d * CAP, CAP), 0:width],
-            dst.at[rows(dp * CAP, CAP), 0:width],
-            ssem.at[i],
-            rsem.at[i],
+            src.at[rows(d * CAP, CAP), cols],
+            dst.at[rows(dp * CAP, CAP), cols],
+            ssem.at[base + i],
+            rsem.at[base + i],
             device_id=(d, mp),
             device_id_type=MESH,
         )
@@ -83,7 +85,7 @@
             return carry
 
         lax.fori_loop(1, NDP, one, 0)
-        dst[rows(dp * CAP, CAP), 0:width] = src[rows(dp * CAP, CAP), 0:width]
+        dst[rows(dp * CAP, CAP), cols] = src[rows(dp * CAP, CAP), cols]
 
     def wait():
         def one(i, carry):
@@ -95,17 +97,21 @@
     return start, wait
 
 
-def ring_gather(src, dst, ssem, rsem, dp, mp, right, left):
-    make = copier(ssem, rsem)
+def ring_gather(src, dst, ssem, rsem, dp, mp, right, left, first_col=0, width=D, base=0):
+    plain = copier(ssem, rsem)
+    cols = pl.ds(first_col, width)
     h = RD // 2
 
+    def make(a, b, n, dev):
+        return plain(a, b, base + n, dev)
+
     def at(dev, half):
-        return dst.at[rows(dev * RD + half * h, h)]
-
-    a0 = make(src.at[0:h], at(mp, 0), 0, (dp, right))
-    b1 = make(src.at[h:RD], at(mp, 1), 1, (dp, left))
-    a1 = make(src.at[h:RD], at(mp, 1), 2, (dp, right))
-    b0 = make(src.at[0:h], at(mp, 0), 3, (dp, left))
+        return dst.at[rows(dev * RD + half * h, h), cols]
+
+    a0 = make(src.at[0:h, cols], at(mp, 0), 0, (dp, right))
+    b1 = make(src.at[h:RD, cols], at(mp, 1), 1, (dp, left))
+    a1 = make(src.at[h:RD, cols], at(mp, 1), 2, (dp, right))
+    b0 = make(src.at[0:h, cols], at(mp, 0), 3, (dp, left))
     f0 = make(at(left, 0), at(left, 0), 4, (dp, right))
     f1 = make(at(right, 1), at(right, 1), 5, (dp, left))
 
@@ -134,19 +140,24 @@
     return start, onward, near, far, drain
 
 
-def ring_reduce(part, ha, hb, fl, fr, ssem, rsem, dp, mp, right, left, opp):
-    make = copier(ssem, rsem)
+def ring_reduce(part, ha, hb, fl, fr, ssem, rsem, dp, mp, right, left, opp, first_col=0, width=D, base=0):
+    plain = copier(ssem, rsem)
+    cols = pl.ds(first_col, width)
+
+    def make(src, dst, n, dev):
+        return plain(src, dst, base + n, dev)
+
     h = RD // 2
 
     def at(dev, half):
-        return part.at[rows(dev * RD + half * h, h)]
-
-    s0 = make(at(opp, 0), ha, 0, (dp, right))
-    s1 = make(at(opp, 1), hb, 1, (dp, left))
-    s2 = make(at(right, 1), fl.at[h:RD], 2, (dp, right))
-    s3 = make(at(left, 0), fr.at[0:h], 3, (dp, left))
-    s4 = make(at(right, 0), fl.at[0:h], 4, (dp, right))
-    s5 = make(at(left, 1), fr.at[h:RD], 5, (dp, left))
+        return part.at[rows(dev * RD + half * h, h), cols]
+
+    s0 = make(at(opp, 0), ha.at[:, cols], 0, (dp, right))
+    s1 = make(at(opp, 1), hb.at[:, cols], 1, (dp, left))
+    s2 = make(at(right, 1), fl.at[h:RD, cols], 2, (dp, right))
+    s3 = make(at(left, 0), fr.at[0:h, cols], 3, (dp, left))
+    s4 = make(at(right, 0), fl.at[0:h, cols], 4, (dp, right))
+    s5 = make(at(left, 1), fr.at[h:RD, cols], 5, (dp, left))
 
     def first():
         s0.start()
@@ -159,11 +170,11 @@
     def onward():
         s0.wait_recv()
         r0 = rows(right * RD, h)
-        part[r0] = (part[r0].astype(F32) + ha[...].astype(F32)).astype(BF)
+        part[r0, cols] = (part[r0, cols].astype(F32) + ha[:, cols].astype(F32)).astype(BF)
         s4.start()
         s1.wait_recv()
         r1 = rows(left * RD + h, h)
-        part[r1] = (part[r1].astype(F32) + hb[...].astype(F32)).astype(BF)
+        part[r1, cols] = (part[r1, cols].astype(F32) + hb[:, cols].astype(F32)).astype(BF)
         s5.start()
 
     def finish():
@@ -191,16 +202,15 @@
 
 
 def head_cols(h):
-    base = h * 3 * HP
-    return [pl.ds(pl.multiple_of(base + k * HP, 128), HP) for k in range(3)]
+    return [pl.ds(pl.multiple_of(k * NH * HP + h * HP, 128), HP) for k in range(3)]
 
 
 def sublayer_kernel(
     packing, coords, seg, prow, pcol, gain, patch_in, w_in, wo_in, cot_in,
     out, dpatch, total,
-    stream, ng, cotg, qkv, datt, idx, sel, wq, wo, crd, segc,
-    send, recv, ret, prob, att, dk, dv, part, dnp, grad,
-    ha, hb, fl, fr, ha2, hb2, fl2, fr2, core_in, ax, az, bx, bz,
+    stream, ng, cotg, qkv, datt, idx, sel, wq, wo, crd,
+    send, recv, ret, prob, att, dk, part, dnp, grad,
+    ha, hb, fl, fr, ha2, hb2, fl2, fr2, core_in, ax, az, bx, bz, stats,
     as_, ar, bs, br, cs, cr, ns, nr, os_, or_, ys, yr, gs, gr, ls, lk,
 ):
     dp, mp, right, left, opp = place()
@@ -240,20 +250,26 @@
         send[at, D:] = mm(pick, ext).astype(BF)
         return carry
 
+    l_c.wait()
+    cot_own = cotg.at[rows(mp * RD, RD)]
+    cg = [
+        ring_gather(cot_own, cotg, cs, cr, dp, mp, right, left, first_col, width, base)
+        for first_col, width, base in ((0, D - CA, 0), (D - CA, CA, 6))
+    ]
+    pl.semaphore_wait(bar, NDP + 1)
+    cg[0][0]()
     lax.fori_loop(0, SLOTS // 128, fill, 0)
-    pl.semaphore_wait(bar, NDP + 1)
-    go, done = a2a_copies(send, recv, as_, ar, dp, mp)
-    go()
-    l_c.wait()
-    c_start, c_onward, c_near, c_far, c_drain = ring_gather(
-        cotg.at[rows(mp * RD, RD)], cotg, cs, cr, dp, mp, right, left
-    )
-    c_start()
+    a2a = [
+        a2a_copies(send, recv, as_, ar, dp, mp, first_col, width, base)
+        for first_col, width, base in ((CA, D + 128 - CA, 0), (0, CA, NDP))
+    ]
+    a2a[0][0]()
+    a2a[1][0]()
 
     crd[:, 0:1] = column(coords[0:1, :])
     crd[:, 1:2] = column(coords[1:2, :])
     for i in range(4):
-        segc[i * 256 : (i + 1) * 256, :] = column(seg[:, i * 256 : (i + 1) * 256])
+        crd[:, 2 + i : 3 + i] = column(seg[:, i * 256 : (i + 1) * 256])
     l_w.wait()
     l_o.wait()
 
@@ -263,7 +279,7 @@
         pick = jnp.where((i1 == i0 + h * HD) & (i0 < HD), 1.0, 0.0).astype(BF)
 
         def one(k, inner):
-            wq[rows(h * 3 * HP + k * HP, HP), :] = mm(pick, grad[k, 0:GW, :]).astype(BF)
+            wq[rows(k * NH * HP + h * HP, HP), :] = mm(pick, grad[k, 0:GW, :]).astype(BF)
             return inner
 
         lax.fori_loop(0, 3, one, 0)
@@ -271,30 +287,46 @@
         return carry
 
     lax.fori_loop(0, NH, pad_head, 0)
-    c_onward()
-    done()
+    cg[0][1]()
+    a2a[0][1]()
     idx[...] = recv[:, D:]
 
-    def unpack(i, carry):
-        at = rows(i * 128, 128)
-        code = recv[:, D:].astype(F32)
-        want = (lax.broadcasted_iota(jnp.int32, (SLOTS, 128), 1) + (i * 128 + 1)).astype(F32)
-        pick = jnp.where(code == want, 1.0, 0.0).astype(BF)
-        packed = mm(pick, recv[:, 0:D], 0, 0)
-        gi = lax.broadcasted_iota(jnp.int32, (128, 16), 1)
-        row_hot = jnp.where(gi == crd[at, 0:1], 1.0, 0.0).astype(BF)
-        col_hot = jnp.where(gi == crd[at, 1:2], 1.0, 0.0).astype(BF)
-        s = (packed + mm(row_hot, prow[...]) + mm(col_hot, pcol[...])).astype(BF)
-        stream[at, :] = s
-        unit, _ = layer_norm(s)
-        ng[rows(mp * RD + i * 128, 128), :] = (unit * gain[...].astype(F32)).astype(BF)
-        return carry
-
-    lax.fori_loop(0, RD // 128, unpack, 0)
-    n_start, n_onward, n_near, n_far, n_drain = ring_gather(
-        ng.at[rows(mp * RD, RD)], ng, ns, nr, dp, mp, right, left
-    )
-    n_start()
+    def unpack(first_col, width):
+        cols = pl.ds(first_col, width)
+
+        def one(i, carry):
+            at = rows(i * 128, 128)
+            code = recv[:, D:].astype(F32)
+            want = (lax.broadcasted_iota(jnp.int32, (SLOTS, 128), 1) + (i * 128 + 1)).astype(F32)
+            pick = jnp.where(code == want, 1.0, 0.0).astype(BF)
+            packed = mm(pick, recv[:, cols], 0, 0)
+            gi = lax.broadcasted_iota(jnp.int32, (128, 16), 1)
+            row_hot = jnp.where(gi == crd[at, 0:1], 1.0, 0.0).astype(BF)
+            col_hot = jnp.where(gi == crd[at, 1:2], 1.0, 0.0).astype(BF)
+            pos = mm(row_hot, prow[:, cols]) + mm(col_hot, pcol[:, cols])
+            stream[at, cols] = (packed + pos).astype(BF)
+            return carry
+
+        lax.fori_loop(0, RD // 128, one, 0)
+
+    sg = [
+        ring_gather(stream, dnp, ns, nr, dp, mp, right, left, first_col, width, base)
+        for first_col, width, base in ((CA, D - CA, 0), (0, CA, 6))
+    ]
+    unpack(CA, D - CA)
+    sg[0][0]()
+    sg[0][1]()
+    a2a[1][1]()
+    unpack(0, CA)
+    sg[1][0]()
+
+    def normalize(s, src, first_row):
+        def one(i, carry):
+            unit, _ = layer_norm(src[rows(first_row + i * 64, 64), 0:D])
+            ng[rows(s * RD + i * 64, 64), :] = (unit * gain[...].astype(F32)).astype(BF)
+            return carry
+
+        lax.fori_loop(0, RD // 64, one, 0)
 
     def project(s):
         def one(n, carry):
@@ -309,18 +341,18 @@
     def back_project(s):
         datt[rows(s * RD, RD), :] = mm(cotg[rows(s * RD, RD)], wo[...], 1, 1).astype(BF)
 
+    normalize(mp, stream, 0)
     project(mp)
-    back_project(mp)
-    c_near()
-    c_far()
-    back_project(right)
-    back_project(left)
-    back_project(opp)
-    n_onward()
-    n_near()
-    project(right)
-    project(left)
-    n_far()
+    sg[1][1]()
+    cg[1][0]()
+    sg[0][2]()
+    sg[1][2]()
+    for s in (right, left):
+        normalize(s, dnp, s * RD)
+        project(s)
+    sg[0][3]()
+    sg[1][3]()
+    normalize(opp, dnp, opp * RD)
     project(opp)
 
     def fwd(h, carry):
@@ -328,12 +360,17 @@
         hc = pl.ds(pl.multiple_of(h * HP, 128), HP)
         for r0, k0, k1, p0 in BLOCKS:
             s = mm(qkv[r0 : r0 + 256, qc], qkv[k0:k1, kc], 1, 1) * scale
-            same = segc[r0 : r0 + 256, :] == seg[:, k0:k1]
+            same = crd[:, 2 + r0 // 256 : 3 + r0 // 256] == seg[:, k0:k1]
             s = jnp.where(same, s, -1e30)
             e = jnp.where(same, jnp.exp(s - jnp.max(s, axis=-1, keepdims=True)), 0.0)
             p = (e / jnp.sum(e, axis=-1, keepdims=True)).astype(BF)
             prob[h, :, p0 : p0 + k1 - k0] = p
             att[r0 : r0 + 256, hc] = mm(p, qkv[k0:k1, vc]).astype(BF)
+
+        @pl.when(h == 1)
+        def _():
+            cg[1][1]()
+
         return carry
 
     lax.fori_loop(0, NH, fwd, 0)
@@ -350,6 +387,11 @@
     out_rows(left)
     second()
     out_rows(mp)
+    for k in range(2):
+        cg[k][2]()
+        cg[k][3]()
+    for s in (mp, right, left, opp):
+        back_project(s)
 
     def dev(zz, xx, cc):
         return ((zz * 4 + xx) * 2 + cc, mp)
@@ -359,11 +401,11 @@
 
     halves = (pl.ds(0, CA), pl.ds(CA, D - CA))
 
-    def piece(h, r, size, cols):
-        return grad.at[2 * c + r // HP, rows(h * HP + lax.rem(r, HP), size), cols]
-
-    def placed_piece(h, r, size, cols):
-        return total.at[2 * c + r // HP, rows(h * HP + lax.rem(r, HP), size), cols]
+    def piece(k, r, size, cols):
+        return grad.at[k, rows(c * RD + r, size), cols]
+
+    def placed_piece(k, r, size, cols):
+        return total.at[k, rows(c * RD + r, size), cols]
 
     class Stage:
         def __init__(self, h):
@@ -379,13 +421,12 @@
             self.make, self.far = make, far
 
         def swap(self):
-            hr = rows(self.h * HP, HP)
             return self.make(
-                grad.at[pl.ds(2 * other, 2), hr], core_in.at[self.h], 0, dev(z, x, other)
+                grad.at[self.h, rows(other * RD, RD)], core_in.at[self.h], 0, dev(z, x, other)
             )
 
         def last(self):
-            ours = total.at[pl.ds(2 * c, 2), rows(self.h * HP, HP)]
+            ours = total.at[self.h, rows(c * RD, RD)]
             return self.make(ours, ours, 25, dev(z, x, other))
 
         def group(self, kind, a):
@@ -422,10 +463,9 @@
         def s1(self):
             h = self.h
             self.swap().wait_recv()
-            hr = rows(h * HP, HP)
-            for k in range(2):
-                mine = grad[2 * c + k, hr, :].astype(F32)
-                grad[2 * c + k, hr, :] = (mine + core_in[h, k].astype(F32)).astype(BF)
+            for i in range(2):
+                r, q = rows(c * RD + i * 128, 128), slice(i * 128, (i + 1) * 128)
+                grad[h, r, :] = (grad[h, r, :].astype(F32) + core_in[h, q].astype(F32)).astype(BF)
             big = self.group(0, 0), self.group(0, 1)
             for s in (1, 0, 2):
                 for a in range(2):
@@ -477,21 +517,30 @@
             for q in sent:
                 q.wait_send()
 
-    def weight_grad(h):
-        hr = rows(h * HP, HP)
-        all3 = pl.ds(pl.multiple_of(h * 3 * HP, 128), 3 * HP)
-        g = (mm(qkv[:, all3], ng[...], 0, 0) * coef).astype(BF)
-        for k in range(3):
-            grad[k, hr, :] = g[k * HP : (k + 1) * HP]
+    st = [Stage(k) for k in range(4)]
+    grad[3] = (mm(att[...], cotg[...], 0, 0) * coef).astype(BF)
+    st[3].s0()
+
+    def bwd_value(h, carry):
         hc = pl.ds(pl.multiple_of(h * HP, 128), HP)
-        grad[3, hr, :] = (mm(att[:, hc], cotg[...], 0, 0) * coef).astype(BF)
-        Stage(h).s0()
+        hc2 = pl.ds(pl.multiple_of(NH * HP + h * HP, 128), HP)
+        dk[...] = jnp.zeros_like(dk)
+        for r0, k0, k1, p0 in BLOCKS:
+            dk[k0:k1, :] += mm(prob[h, :, p0 : p0 + k1 - k0], datt[r0 : r0 + 256, hc], 0, 0)
+        recv[:, hc] = dk[0:512, :].astype(BF)
+        recv[:, hc2] = dk[512:SEQ, :].astype(BF)
+        return carry
+
+    lax.fori_loop(0, NH, bwd_value, 0)
+    d_value = mm(recv[:, 0:512], ng[0:512], 0, 0) + mm(recv[:, 512:1024], ng[512:SEQ], 0, 0)
+    grad[2] = (d_value * coef).astype(BF)
+    st[2].s0()
+    st[3].s1()
 
     def bwd(h, carry):
         qc, kc, vc = head_cols(h)
         hc = pl.ds(pl.multiple_of(h * HP, 128), HP)
         dk[...] = jnp.zeros_like(dk)
-        dv[...] = jnp.zeros_like(dv)
         for r0, k0, k1, p0 in BLOCKS:
             p = prob[h, :, p0 : p0 + k1 - k0]
             da = datt[r0 : r0 + 256, hc]
@@ -501,102 +550,155 @@
             dprob = mm(da, qkv[k0:k1, vc], 1, 1)
             ds = (p.astype(F32) * (dprob - delta) * scale).astype(BF)
             dk[k0:k1, :] += mm(ds, qkv[r0 : r0 + 256, qc], 0, 0)
-            dv[k0:k1, :] += mm(p, da, 0, 0)
             qkv[r0 : r0 + 256, qc] = mm(ds, qkv[k0:k1, kc]).astype(BF)
         qkv[:, kc] = dk[...].astype(BF)
-        qkv[:, vc] = dv[...].astype(BF)
-
-        @pl.when(h >= 1)
+        hc2 = pl.ds(pl.multiple_of(NH * HP + h * HP, 128), HP)
+        qkv[0:512, vc] = recv[:, hc]
+        qkv[512:SEQ, vc] = recv[:, hc2]
+
+        @pl.when(h == 0)
         def _():
-            weight_grad(h - 1)
-
-        @pl.when(h >= 2)
-        def _():
-            Stage(h - 2).s1()
+            st[2].s1()
 
         @pl.when(h == 1)
         def _():
             onward()
+            st[3].s2()
+
+        @pl.when(h == 2)
+        def _():
+            st[2].s2()
+            st[3].s3()
 
         @pl.when(h == 3)
         def _():
-            Stage(h - 3).s2()
+            st[3].s4()
+            st[2].s3()
 
         return carry
 
     lax.fori_loop(0, NH, bwd, 0)
-    first2, second2, onward2, finish2, drain2 = ring_reduce(
-        dnp, ha2, hb2, fl2, fr2, ys, yr, dp, mp, right, left, opp
-    )
+
+    def weight_grad(k):
+        cols = pl.ds(k * NH * HP, NH * HP)
+        grad[k] = (mm(qkv[:, cols], ng[...], 0, 0) * coef).astype(BF)
+        st[k].s0()
+
+    sg[0][4]()
+    sg[1][4]()
+    rs = [
+        ring_reduce(
+            dnp, ha2, hb2, fl2, fr2, ys, yr, dp, mp, right, left, opp, first_col, width, base
+        )
+        for first_col, width, base in ((0, HP + CA, 0), (HP + CA, D - CA, 6))
+    ]
 
     def d_rows(s):
-        dnp[rows(s * RD, RD), :] = mm(qkv[rows(s * RD, RD), :], wq[...]).astype(BF)
+        def one(i, carry):
+            r = rows(s * RD + i * 128, 128)
+            v = mm(qkv[r, :], wq[...])
+            dnp[r, HP:] = v.astype(BF)
+            m1 = jnp.sum(v * gain[...].astype(F32), axis=-1, keepdims=True) * (1.0 / D)
+            m2 = jnp.sum(v * ng[r, :].astype(F32), axis=-1, keepdims=True) * (1.0 / D)
+            lane = lax.broadcasted_iota(jnp.int32, (128, HP), 1)
+            dnp[r, 0:HP] = jnp.where(lane < HP // 2, m1, m2).astype(BF)
+            return carry
+
+        lax.fori_loop(0, 2, one, 0)
 
     d_rows(opp)
-    first2()
+    rs[0][0]()
     d_rows(right)
     d_rows(left)
-    second2()
-    weight_grad(3)
+    rs[0][1]()
+    rs[1][0]()
+    rs[1][1]()
+    weight_grad(0)
+    weight_grad(1)
     d_rows(mp)
-    st = [Stage(h) for h in range(NH)]
-    st[2].s1()
-    onward2()
-    st[1].s2()
-    st[0].s3()
-    st[3].s1()
+    st[2].s4()
+    st[3].s5()
+    rs[0][2]()
+    st[0].s1()
+    st[1].s1()
+    rs[1][2]()
     finish()
     acc = part[rows(mp * RD, RD)].astype(F32) + fl[...].astype(F32) + fr[...].astype(F32)
     part[rows(mp * RD, RD)] = (stream[...].astype(F32) + acc).astype(BF)
     l_out = pltpu.make_async_copy(part.at[rows(mp * RD, RD)], out, ls.at[8])
     l_out.start()
-    st[2].s2()
+    st[2].s5()
+    back = send
+
+    def ln_stats(i, carry):
+        r = rows(i * 64, 64)
+        sf = stream[r, :].astype(F32)
+        mean = jnp.mean(sf, axis=-1, keepdims=True)
+        cen = sf - mean
+        stats[r, 0:1] = mean
+        stats[r, 1:2] = lax.rsqrt(jnp.mean(cen * cen, axis=-1, keepdims=True) + 1e-06)
+        return carry
+
+    lax.fori_loop(0, RD // 64, ln_stats, 0)
+
+    def total_of(i, cols):
+        r = rows(i * 64, 64)
+        own = dnp[rows(mp * RD + i * 64, 64), cols].astype(F32)
+        return own + fl2[r, cols].astype(F32) + fr2[r, cols].astype(F32)
+
+    def chunk(first_col, width):
+        here, there = pl.ds(first_col, width), pl.ds(HP + first_col, width)
+
+        def ln_back(i, carry):
+            r = rows(i * 64, 64)
+            if first_col == 0:
+                both = total_of(i, pl.ds(0, HP))
+                stats[r, 2:3] = both[:, 0:1]
+                stats[r, 3:4] = both[:, HP // 2 : HP // 2 + 1]
+            inv = stats[r, 1:2]
+            unit = (stream[r, here].astype(F32) - stats[r, 0:1]) * inv
+            e = total_of(i, there) * gain[:, here].astype(F32)
+            dst = cotg[rows(mp * RD + i * 64, 64), here].astype(F32) + inv * (
+                e - stats[r, 2:3] - unit * stats[r, 3:4]
+            )
+            stream[r, here] = dst.astype(BF)
+            return carry
+
+        lax.fori_loop(0, RD // 64, ln_back, 0)
+
+        def spread(i, carry):
+            r = rows(i * 128, 128)
+            code = idx[r, :].astype(F32)
+            want = (lax.broadcasted_iota(jnp.int32, (128, 128), 1) + 1).astype(F32)
+            lo = jnp.where(code == want, 1.0, 0.0).astype(BF)
+            hi = jnp.where(code == want + 128.0, 1.0, 0.0).astype(BF)
+            back[r, here] = (mm(lo, stream[0:128, here]) + mm(hi, stream[128:256, here])).astype(BF)
+            return carry
+
+        lax.fori_loop(0, SLOTS // 128, spread, 0)
+
+    backs = [
+        a2a_copies(back, ret, bs, br, dp, mp, first_col, width, base)
+        for first_col, width, base in ((0, CA, 0), (CA, D - CA, NDP))
+    ]
+    st[0].s2()
+    st[1].s2()
+    rs[0][3]()
+    chunk(0, CA)
+    backs[0][0]()
+    st[3].s6()
+    st[0].s3()
     st[1].s3()
+    rs[1][3]()
+    chunk(CA, D - CA)
+    backs[1][0]()
+    st[2].s6()
     st[0].s4()
-    st[3].s2()
-    st[2].s3()
     st[1].s4()
     st[0].s5()
-    finish2()
-    back = send
-    go_back, done_back = a2a_copies(back, ret, bs, br, dp, mp, D)
-
-    def ln_back(i, carry):
-        r = rows(i * 64, 64)
-        unit, inv = layer_norm(stream[r, :])
-        dn = dnp[rows(mp * RD + i * 64, 64), :].astype(F32)
-        e = (dn + fl2[r, :].astype(F32) + fr2[r, :].astype(F32)) * gain[...].astype(F32)
-        dst = cotg[rows(mp * RD + i * 64, 64), :].astype(F32) + inv * (
-            e
-            - jnp.mean(e, axis=-1, keepdims=True)
-            - unit * jnp.mean(e * unit, axis=-1, keepdims=True)
-        )
-        stream[r, :] = dst.astype(BF)
-        return carry
-
-    lax.fori_loop(0, RD // 64, ln_back, 0)
-
-    def spread(i, carry):
-        r = rows(i * 128, 128)
-        code = idx[r, :].astype(F32)
-        want = (lax.broadcasted_iota(jnp.int32, (128, 128), 1) + 1).astype(F32)
-        lo = jnp.where(code == want, 1.0, 0.0).astype(BF)
-        hi = jnp.where(code == want + 128.0, 1.0, 0.0).astype(BF)
-        back[r, 0:D] = (mm(lo, stream[0:128, :]) + mm(hi, stream[128:256, :])).astype(BF)
-        return carry
-
-    lax.fori_loop(0, SLOTS // 128, spread, 0)
-    go_back()
-    st[3].s3()
-    st[2].s4()
     st[1].s5()
-    st[0].s6()
-    st[3].s4()
-    st[2].s5()
-    st[1].s6()
-    st[3].s5()
-    st[2].s6()
-    done_back()
+    backs[0][1]()
+    backs[1][1]()
 
     def collect(i, carry):
         r = rows(i * 128, 128)
@@ -607,17 +709,19 @@
     lax.fori_loop(0, RD // 128, collect, 0)
     l_dp = pltpu.make_async_copy(recv.at[0:RD, 0:D], dpatch, ls.at[9])
     l_dp.start()
-    st[3].s6()
+    st[0].s6()
+    st[1].s6()
 
     def settle(h, carry):
         Stage(h).s7()
         return carry
 
     lax.fori_loop(0, NH, settle, 0)
-    c_drain()
-    n_drain()
+    cg[0][4]()
+    cg[1][4]()
     drain()
-    drain2()
+    rs[0][4]()
+    rs[1][4]()
     l_out.wait()
     l_dp.wait()
 
@@ -647,17 +751,19 @@
         scratch_shapes=[
             vm(RD, D), vm(SEQ, D), vm(SEQ, D), vm(SEQ, NH * 3 * HP), vm(SEQ, NH * HP),
             vm(SLOTS, 128), vm(SLOTS, RD), vm(NH * 3 * HP, D), vm(NH * HP, D),
-            pltpu.VMEM((RD, 2), jnp.int32), pltpu.VMEM((SEQ, 1), jnp.int32),
+            pltpu.VMEM((RD, 6), jnp.int32),
             vm(SLOTS, D + 128), vm(SLOTS, D + 128), vm(SLOTS, D),
             vm(NH, 256, 2048), vm(SEQ, NH * HP),
-            pltpu.VMEM((SEQ, HP), F32), pltpu.VMEM((SEQ, HP), F32),
-            vm(SEQ, D), vm(SEQ, D), vm(4, NH * HP, D),
+            pltpu.VMEM((SEQ, HP), F32),
+            vm(SEQ, D), vm(SEQ, D + HP), vm(4, NH * HP, D),
             vm(h, D), vm(h, D), vm(RD, D), vm(RD, D),
-            vm(h, D), vm(h, D), vm(RD, D), vm(RD, D),
-            vm(NH, 2, HP, D),
+            vm(h, D + HP), vm(h, D + HP), vm(RD, D + HP), vm(RD, D + HP),
+            vm(NH, RD, D),
             vm(NH, 3, 64, CA), vm(NH, 3, 16, CA), vm(NH, 3, 64, D - CA), vm(NH, 3, 16, D - CA),
-            dma(NDP), dma(NDP), dma(NDP), dma(NDP), dma(6), dma(6), dma(6), dma(6),
-            dma(6), dma(6), dma(6), dma(6), dma(NH, 26), dma(NH, 26), dma(10), dma(NH, 2),
+            pltpu.VMEM((RD, 4), F32),
+            dma(2 * NDP), dma(2 * NDP), dma(2 * NDP), dma(2 * NDP),
+            dma(12), dma(12), dma(12), dma(12),
+            dma(6), dma(6), dma(12), dma(12), dma(NH, 26), dma(NH, 26), dma(10), dma(NH, 2),
         ],
         compiler_params=pltpu.CompilerParams(
             collective_id=0, has_side_effects=True, vmem_limit_bytes=60 * 2**20

time: 191 us -> 185 us (0.969)
  Pallas kernels: 178 us -> 172 us
    pallas_call x1, Pallas kernels: 178 us -> 172 us  [local(): pl.pallas_call(sublayer_kernel, out_shape=(sds(RD, D), sds(RD, D), sds(4,...]
where the time goes in v3:
time: 185 us
  Pallas kernels  172 us (93%)
  local copies, waits for them, and re-layouts  12.4 us (7%)
    pallas_call x1, Pallas kernels, local(): pl.pallas_call(sublayer_kernel, out_shape=(sds(RD, D), sds(RD, D), sds(4,...  172 us
    slice x1, local copies, waits for them, and re-layouts, local(): grad_qkv = wide[:3, :, :HD].reshape(3, GW, D).transpose(2, 0, 1)  6.2 us

profile of v3, /device:TPU:1, one launch (start us, length us, event | category | flops | bytes accessed | tf_op | source)
XLA Modules:
  0.0 184.8 jit_solution(10689272294815391274)
XLA Ops:
  0.6 1.3 reshape.21.gain
  1.9 171.8 %sublayer.1 = (bf16[256,1664]{1,0:T(8,128)(2,1)}, bf16[256,1664]{1,0:T(8,128)(2,1)}, bf16[4,512,1664]{2,1,0:T(8,128)(2,1)}) custom-call(s32[2,256]{1,0:T(2,128)} %packing.1, s32[2,256]{1,0:T(2,128)} %coords.1, s32[1,1024]{1,0:T(1,128)} %bitcast.13, bf16[16,1664]{1,0:T(8,128)(2,1)} %prow.1, bf16[16,1664]{1,0:T(8,128)(2,1)} %pcol.1, ...), custom_call_target="tpu_custom_call" | custom-call | tf_op jit(solution)/shard_map/sublayer/pallas_call | solution.py:746
  173.8 3.1 %slice.9 = f32[1,4,104,1664]{3,2,1,0:T(8,128)} slice(bf16[4,4,128,1664]{3,2,1,0:T(8,128)(2,1)} %bitcast.8), slice={[3:4], [0:4], [0:104], [0:1664]} | slice | bytes 5537792 | tf_op jit(solution)/shard_map/slice | solution.py:778
  176.8 0.0 copy-start.1
  176.8 0.0 copy-start
  176.8 6.2 %slice.8 = f32[3,4,104,1664]{3,2,1,0:T(8,128)} slice(bf16[4,4,128,1664]{3,2,1,0:T(8,128)(2,1)} %bitcast.9), slice={[0:3], [0:4], [0:104], [0:1664]} | slice | bytes 16613376 | tf_op jit(solution)/shard_map/slice | solution.py:777
  183.0 0.0 copy-done.1
  183.0 0.9 copy.16
  183.9 0.0 copy-done
  183.9 0.9 copy.17
Async XLA Ops:
  176.8 6.2 %copy-start.1 = (bf16[256,1664]{1,0:T(8,128)(2,1)S(1)}, bf16[256,1664]{1,0:T(8,128)(2,1)}, u32[]{:S(2)}) copy-start(bf16[256,1664]{1,0:T(8,128)(2,1)} %get-tuple-element.14) | copy-start | bytes 2555908
  176.8 7.1 %copy-start = (bf16[256,1664]{1,0:T(8,128)(2,1)S(1)}, bf16[256,1664]{1,0:T(8,128)(2,1)}, u32[]{:S(2)}) copy-start(bf16[256,1664]{1,0:T(8,128)(2,1)} %get-tuple-element.15) | copy-start | bytes 2555908
